TPU v7x, 512 devices: a whole 4x8x8 slice. The times are simulated.
512 devices in a mesh: pipe: 4 (over x), tensor: 32 (over z, y_lo), dp: 4 (over y_hi, core).
Axes of the slice: x: 4, y: 8 (y_hi: 2, y_lo: 4; y = y_hi * 4 + y_lo), z: 8, core: 2. Of those that a mesh axis runs over, the one named last changes fastest.
Arguments:
- stash: bfloat16 [4096, 29568], P(('pipe', 'dp'), 'tensor'), may hold values from -6 to 6
- out_grads: bfloat16 [4096, 8192], P(('pipe', 'dp'), 'tensor'), may hold values from -0.09375 to 0.09375
- block_counts: int32 [16], replicated, may hold values from 1 to 2
Outputs:
- weight_grad: bfloat16 [29568, 8192], P('tensor', ('pipe', 'dp'))
Inputs may be any that keep to these rules, and one draw needn't show every extreme that they name: `block_counts`: each micro-batch has at least one live block; some micro-batch has all 2.
All inputs are finite; a program needn't handle non-finite values.
Results may differ from a plain program's by a relative error of at most 0.001.
Values may be sent and summed in bfloat16 or wider, within the bound.
No kernel may reach another device: no remote copies, remote signals or barrier semaphores. Data moves between devices by JAX's collectives and lax.ppermute only.
A program may use at most 64 MiB of HBM per device.

v0:
```python
import jax
import jax.numpy as jnp
from jax import lax
from jax.sharding import PartitionSpec as P

ROWBLK = 128
BLK = 2


def zero_dead(grads, counts):
    micro_rows = BLK * ROWBLK
    number = grads.shape[0] // micro_rows
    shaped = grads.reshape(number, micro_rows, grads.shape[1])
    slots = jnp.arange(micro_rows, dtype=jnp.int32)
    alive = slots[None, :] < ROWBLK * counts[:, None]
    return jnp.where(alive[:, :, None], shaped, jnp.zeros_like(shaped)).reshape(grads.shape)


def shards(stash, out_grads, block_counts):
    wide = lax.all_gather(out_grads, "tensor", axis=1, tiled=True)
    owned = lax.all_to_all(wide, ("pipe", "dp"), split_axis=1, concat_axis=0, tiled=True)
    owned = zero_dead(owned, block_counts)
    summed = lax.dot_general(
        lax.all_gather(stash, ("pipe", "dp"), axis=0, tiled=True),
        owned,
        (((0,), (0,)), ((), ())),
        preferred_element_type=jnp.float32,
    )
    return summed.astype(jnp.bfloat16)


def solution(mesh):
    placed = (P(("pipe", "dp"), "tensor"), P(("pipe", "dp"), "tensor"), P())
    return jax.shard_map(
        shards, mesh=mesh, in_specs=placed, out_specs=P("tensor", ("pipe", "dp")), check_vma=False
    )
```

profile of v0, /device:TPU:49, one launch (start us, length us, event | category | flops | bytes accessed | tf_op | source)
XLA Modules:
  0.0 371.3 jit_solution(11864328366536849484)
XLA Ops:
  6.5 0.0 all-gather.3.cloned.1.call-start
  6.5 1.7 copy.4
  8.2 0.0 all-gather.3.cloned.1.call-update
  8.2 0.0 all-gather.5.cloned.1.call-start
  8.3 0.7 all-gather.5.cloned.1.call-update
  9.0 148.7 %all-gather.3.cloned.1.call-done = bf16[256,8192]{0,1:T(8,128)(2,1)} async-done(((bf16[256,256]{0,1:T(8,128)(2,1)}), bf16[256,8192]{0,1:T(8,128)(2,1)}) %all-gather.3.cloned.1.call-update) | async-done | bytes 4194320 | tf_op jit(solution)/shard_map/all_gather | solution.py:20
  157.7 0.0 copy-start
  157.7 30.7 %all-to-all-start = ((bf16[256,16,512]{0,2,1:T(8,128)(2,1)}), bf16[256,16,512]{0,2,1:T(8,128)(2,1)}, u32[]{:S(2)}, u32[]{:S(2)}) async-start(bf16[256,16,512]{0,2,1:T(8,128)(2,1)} %bitcast.8), calls=%async_computation | async-start | bytes 8388608 | tf_op jit(solution)/shard_map/all_to_all | solution.py:21
  188.4 0.0 copy-done
  188.4 0.1 iota_compare_fusion
  188.5 62.8 %all-to-all-done = bf16[256,16,512]{0,2,1:T(8,128)(2,1)} async-done(((bf16[256,16,512]{0,2,1:T(8,128)(2,1)}), bf16[256,16,512]{0,2,1:T(8,128)(2,1)}, u32[]{:S(2)}, u32[]{:S(2)}) %all-to-all-start) | async-done | bytes 4194336 | tf_op jit(solution)/shard_map/all_to_all | solution.py:21
  251.3 6.4 %copy.5 = bf16[16,256,512]{2,1,0:T(8,128)(2,1)} copy(bf16[16,256,512]{1,2,0:T(8,128)(2,1)} %bitcast.1) | data formatting | bytes 8388608 | tf_op jit(solution)/shard_map/all_to_all | solution.py:21
  257.7 4.0 %bitcast_select_fusion = bf16[4096,512]{1,0:T(8,128)(2,1)} fusion(bf16[16,256,512]{2,1,0:T(8,128)(2,1)} %copy.5, pred[4096]{0:T(1024)(128)(4,1)S(1)} %lt.23), kind=kLoop, calls=%fused_computation | loop fusion | flops 2097152 | bytes 8392704 | tf_op jit(solution)/shard_map/jit(_where)/select_n | solution.py:16
  261.7 93.3 %all-gather.5.cloned.1.call-done = bf16[4096,924]{0,1:T(8,128)(2,1)} async-done(((bf16[256,924]{0,1:T(8,128)(2,1)}), bf16[4096,924]{0,1:T(8,128)(2,1)}) %all-gather.5.cloned.1.call-update) | async-done | bytes 7569424 | tf_op jit(solution)/shard_map/all_gather | solution.py:24
  355.0 9.5 %fusion = bf16[924,512]{1,0:T(8,128)(2,1)} fusion(bf16[4096,512]{1,0:T(8,128)(2,1)} %bitcast_select_fusion, bf16[4096,924]{0,1:T(8,128)(2,1)} %all-gather.5.cloned.1.call-done), kind=kOutput, calls=%fused_computation.2 | convolution fusion | flops 3876009984 | bytes 12709888 | tf_op jit(solution)/shard_map/dot_general | solution.py:23
  (2 shorter events, 0.0 us)
Async XLA Ops:
  6.5 151.1 %all-gather.3.cloned.1.call-start = ((), (), s32[]{:S(2)}) async-start(), calls=%async_computation.1 | async-start | bytes 4325376 | tf_op jit(solution)/shard_map/all_gather | solution.py:20
  8.2 346.8 %all-gather.5.cloned.1.call-start = ((), (), s32[]{:S(2)}) async-start(), calls=%async_computation.2 | async-start | bytes 8077312 | tf_op jit(solution)/shard_map/all_gather | solution.py:24
  157.7 30.7 %copy-start = (s32[16]{0:T(128)S(1)}, s32[16]{0:T(128)}, u32[]{:S(2)}) copy-start(s32[16]{0:T(128)} %param.5) | copy-start | bytes 196
  157.7 93.6 %all-to-all-start = ((bf16[256,16,512]{0,2,1:T(8,128)(2,1)}), bf16[256,16,512]{0,2,1:T(8,128)(2,1)}, u32[]{:S(2)}, u32[]{:S(2)}) async-start(bf16[256,16,512]{0,2,1:T(8,128)(2,1)} %bitcast.8), calls=%async_computation | async-start | bytes 8388608 | tf_op jit(solution)/shard_map/all_to_all | solution.py:21
Sparse Core Ops, SparseCore 0:
  9.4 148.1 all-gather.2
  160.8 194.1 all-gather.4
where the time goes:
time: 372 us; the launch traced here: 371 us
  waiting for transfers between devices  305 us (82%)
  starting transfers between devices  30.8 us (8%)
  between operations  13.4 us (4%)
  matrix products  9.45 us (3%)
  local copies, waits for them, and re-layouts  8.09 us (2%)
  other arithmetic  4.07 us (1%)
    all_gather x1, waiting for transfers between devices, shards(): wide = lax.all_gather(out_grads, 'tensor', axis=1, tiled=True)  149 us
    all_gather x1, waiting for transfers between devices, shards(): lax.all_gather(stash, ('pipe', 'dp'), axis=0, tiled=True)  93.3 us
    all_to_all x1, waiting for transfers between devices, shards(): lax.all_to_all(wide, ('pipe', 'dp'), split_axis=1, concat_axis=0, tiled=T...  62.8 us
    all_to_all x1, starting transfers between devices, shards(): lax.all_to_all(wide, ('pipe', 'dp'), split_axis=1, concat_axis=0, tiled=T...  30.7 us
    dot_general x1, matrix products, shards(): lax.dot_general(lax.all_gather(stash, ('pipe', 'dp'), axis=0, tiled=True)...  9.45 us
  transfers between devices with their start and end apart: 3, of which 3 were waited for; matrix products, arithmetic and copies ran while one was open for 3% of the time, Pallas kernels for 0%

commit v1 on v0

v1 whole, which is shorter than its diff:
```python
import itertools

import jax
import jax.numpy as jnp
from jax import lax
from jax.experimental import pallas as pl
from jax.experimental.pallas import tpu as pltpu
from jax.sharding import Mesh, PartitionSpec as P

ROWBLK = 128
MROWS = 256
NX, NZ, NYL, NYH, NC = 4, 8, 4, 2, 2
ALL = ("x", "z", "yl", "yh", "c")
PLACES = list(itertools.product(range(NX), range(NZ), range(NYL), range(NYH), range(NC)))


def linear(x, z, yl, yh, c):
    return (((x * NZ + z) * NYL + yl) * NYH + yh) * NC + c


def permute(value, target):
    return lax.ppermute(value, ALL, [(linear(*p), linear(*target(*p))) for p in PLACES])


def to_owner_plane(x, z, yl, yh, c):
    return z // 2, z ^ (2 * x + yh), 2 * c + yl % 2, z % 2, yl // 2


def product(zi, own, yh, s_own, s_par, pieces):
    width, rows = s_own.shape[0], 2 * MROWS
    cols = 2 * pieces[0].shape[-1]
    n = len(pieces)

    def kernel(where, s_own_ref, s_par_ref, *refs):
        g_refs, out_ref, s_vm, g_vm, acc, s_sem, g_sem = refs[:n], *refs[n:]
        z0, own0, yh0 = where[0], where[1], where[2]
        copies = []
        for x in range(NX):
            for ref, half in ((s_own_ref, yh0), (s_par_ref, 1 - yh0)):
                q = 2 * x + half
                copy = pltpu.make_async_copy(ref.at[:, pl.ds(x * rows, rows)], s_vm.at[q], s_sem)
                copy.start()
                copies.append(copy)
        for k, ref in enumerate(g_refs):
            for b in range(NYL):
                copy = pltpu.make_async_copy(
                    ref.at[b],
                    g_vm.at[k, pl.ds((b // 2) * MROWS, MROWS), pl.ds((b % 2) * MROWS, MROWS)],
                    g_sem,
                )
                copy.start()
                copies.append(copy)
        for copy in copies:
            copy.wait()
        for k in range(n):
            q = lax.rem(z0 + k, NZ) ^ own0
            part = jnp.dot(s_vm[q], g_vm[k], preferred_element_type=jnp.float32)
            if k == 0:
                acc[...] = part
            elif k < n - 1:
                acc[...] += part
            else:
                out_ref[...] = (acc[...] + part).astype(out_ref.dtype)

    return pl.pallas_call(
        kernel,
        out_shape=jax.ShapeDtypeStruct((width, cols), jnp.bfloat16),
        in_specs=[pl.BlockSpec(memory_space=pltpu.SMEM)] + [pl.BlockSpec(memory_space=pl.ANY)] * (2 + n),
        out_specs=pl.BlockSpec(memory_space=pltpu.VMEM),
        scratch_shapes=[
            pltpu.VMEM((NZ, width, rows), jnp.bfloat16),
            pltpu.VMEM((NZ, rows, cols), jnp.bfloat16),
            pltpu.VMEM((width, cols), jnp.float32),
            pltpu.SemaphoreType.DMA,
            pltpu.SemaphoreType.DMA,
        ],
        compiler_params=pltpu.CompilerParams(vmem_limit_bytes=48 << 20),
        cost_estimate=pl.CostEstimate(flops=2 * width * NZ * rows * cols, bytes_accessed=12 << 20, transcendentals=0),
    )(jnp.stack([zi, own, yh]).astype(jnp.int32), s_own, s_par, *pieces)


def shards(stash, out_grads, block_counts):
    xi, zi, yh, c = (lax.axis_index(a) for a in ("x", "z", "yh", "c"))
    micro = (xi * NYH + yh) * NC + c

    slots = jnp.arange(MROWS, dtype=jnp.int32)
    alive = slots < ROWBLK * block_counts[micro]
    grads = jnp.where(alive[:, None], out_grads, jnp.zeros_like(out_grads))

    near = permute(grads, to_owner_plane)
    partner = lax.ppermute(stash, "yh", [(0, 1), (1, 0)])
    s_own = lax.all_gather(stash, ("x", "c"), axis=0, tiled=True)
    s_par = lax.all_gather(partner, ("x", "c"), axis=0, tiled=True)

    piece = lax.all_gather(near, "yl", axis=0, tiled=False)
    up = [(i, (i + 1) % NZ) for i in range(NZ)]
    down = [(i, (i - 1) % NZ) for i in range(NZ)]
    below, above = [piece], [piece]
    for _ in range(3):
        below.append(lax.ppermute(below[-1], "z", up))
        above.append(lax.ppermute(above[-1], "z", down))
    last = jnp.where(c == 0, below[3], above[3])
    far = permute(last, lambda x, z, yl, yh, c: (x, (z + 1 - 2 * c) % NZ, yl, yh, c))
    pieces = [piece, above[1], above[2], above[3], far, below[3], below[2], below[1]]
    return product(zi, 2 * xi + yh, yh, s_own.T, s_par.T, pieces)


def solution(mesh):
    fine = Mesh(mesh.devices.reshape(NX, NZ, NYL, NYH, NC), ALL)
    rows, features = ("x", "yh", "c"), ("z", "yl")
    placed = (P(rows, features), P(rows, features), P())
    return jax.shard_map(shards, mesh=fine, in_specs=placed, out_specs=P(features, rows), check_vma=False)
```

time: 372 us -> 152 us (0.41)
  the two profiles are of different devices: /device:TPU:49 before, /device:TPU:26 now
where the time goes in v1:
time: 152 us
  waiting for transfers between devices  61.9 us (41%)
  starting transfers between devices  43.2 us (28%)
  blocking collectives  19.4 us (13%)
  between operations  14.2 us (9%)
  Pallas kernels  9.08 us (6%)
  local copies, waits for them, and re-layouts  2.07 us (1%)
  other arithmetic  1.94 us (1%)
    ppermute x3, waiting for transfers between devices, shards(): below.append(lax.ppermute(below[-1], 'z', up))  23.9 us
    ppermute x3, starting transfers between devices, shards(): above.append(lax.ppermute(above[-1], 'z', down))  21.2 us
    ppermute x1, waiting for transfers between devices, shards(): partner = lax.ppermute(stash, 'yh', [(0, 1), (1, 0)])  20.8 us
    all_gather x1, blocking collectives, shards(): piece = lax.all_gather(near, 'yl', axis=0, tiled=False)  19.4 us
    ppermute x2, waiting for transfers between devices, permute(): lax.ppermute(value, ALL, [(linear(*p), linear(*target(*p))) for p in PLAC...  14.9 us
    ppermute x3, starting transfers between devices, shards(): below.append(lax.ppermute(below[-1], 'z', up))  10.1 us
    pallas_call x1, Pallas kernels, product(): pl.pallas_call(kernel, out_shape=jax.ShapeDtypeStruct((width, cols), jnp....  9.08 us
    ppermute x2, starting transfers between devices, permute(): lax.ppermute(value, ALL, [(linear(*p), linear(*target(*p))) for p in PLAC...  6.89 us
  transfers between devices with their start and end apart: 11, of which 7 were waited for; matrix products, arithmetic and copies ran while one was open for 2% of the time, Pallas kernels for 0%

profile of v1, /device:TPU:26, one launch (start us, length us, event | category | flops | bytes accessed | tf_op | source)
XLA Modules:
  0.0 151.8 jit_solution(4050088131749272566)
XLA Ops:
  6.5 0.0 all-gather.4.cloned.1.call-start
  6.5 0.7 all-gather.4.cloned.1.call-update
  7.3 0.0 all-gather.6.cloned.1.call-start
  7.3 5.0 %collective-permute-start = (bf16[256,924]{0,1:T(8,128)(2,1)}, bf16[256,924]{0,1:T(8,128)(2,1)S(1)}, u32[]{:S(2)}, u32[]{:S(2)}) collective-permute-start(bf16[256,924]{0,1:T(8,128)(2,1)} %param.3), channel_id=1, source_target_pairs={{0,2},{2,0},{1,3},{3,1},{4,6},{6,4},{5,7},{7,5},{8,10},{10,8},{9,1... | collective-permute-start | bytes 1419272 | tf_op jit(solution)/shard_map/ppermute | solution.py:91
  12.3 20.8 %collective-permute-done = bf16[256,924]{0,1:T(8,128)(2,1)S(1)} collective-permute-done((bf16[256,924]{0,1:T(8,128)(2,1)}, bf16[256,924]{0,1:T(8,128)(2,1)S(1)}, u32[]{:S(2)}, u32[]{:S(2)}) %collective-permute-start) | collective-permute-done | bytes 473120 | tf_op jit(solution)/shard_map/ppermute | solution.py:91
  33.1 0.0 copy-start
  33.1 0.8 copy-done
  34.0 0.0 all-gather.6.cloned.1.call-update
  34.0 1.2 dynamic_slice.3
  35.9 1.0 broadcast_select_fusion.1
  36.9 5.0 %collective-permute-start.1 = (bf16[256,256]{1,0:T(8,128)(2,1)S(1)}, bf16[256,256]{1,0:T(8,128)(2,1)S(1)}, u32[]{:S(2)}, u32[]{:S(2)}) collective-permute-start(bf16[256,256]{1,0:T(8,128)(2,1)S(1)} %broadcast_select_fusion.1), channel_id=1, source_target_pairs={{0,0},{1,8},{2,16},{3,24},{4,4},{5,12},{6,20},{7,28},{8,1},{9,9},{... | collective-permute-start | bytes 393224 | tf_op jit(solution)/shard_map/ppermute | solution.py:22
  41.9 4.0 %collective-permute-done.1 = bf16[256,256]{1,0:T(8,128)(2,1)S(1)} collective-permute-done((bf16[256,256]{1,0:T(8,128)(2,1)S(1)}, bf16[256,256]{1,0:T(8,128)(2,1)S(1)}, u32[]{:S(2)}, u32[]{:S(2)}) %collective-permute-start.1) | collective-permute-done | bytes 131104 | tf_op jit(solution)/shard_map/ppermute | solution.py:22
  45.9 19.4 %all-gather = bf16[1024,256]{1,0:T(8,128)(2,1)S(1)} all-gather(bf16[256,256]{1,0:T(8,128)(2,1)S(1)} %collective-permute-done.1), channel_id=2, replica_groups=mesh['x'=4,'z'=8,'yl'=4,'yh'=2,'c'=2] {'yl'}, dimensions={0}, use_global_device_ids=true | all-gather | bytes 655360 | tf_op jit(solution)/shard_map/all_gather | solution.py:95
  65.3 6.3 %collective-permute-start.5 = (bf16[4,256,256]{2,1,0:T(8,128)(2,1)S(1)}, bf16[4,256,256]{2,1,0:T(8,128)(2,1)S(1)}, u32[]{:S(2)}, u32[]{:S(2)}) collective-permute-start(bf16[4,256,256]{2,1,0:T(8,128)(2,1)S(1)} %bitcast.7), channel_id=1, source_target_pairs={{0,16},{16,32},{32,48},{48,64},{64,80},{80,96},{96,112},{112,0},{1... | collective-permute-start | bytes 1572872 | tf_op jit(solution)/shard_map/ppermute | solution.py:100
  71.6 10.9 %collective-permute-start.2 = (bf16[4,256,256]{2,1,0:T(8,128)(2,1)S(1)}, bf16[4,256,256]{2,1,0:T(8,128)(2,1)S(1)}, u32[]{:S(2)}, u32[]{:S(2)}) collective-permute-start(bf16[4,256,256]{2,1,0:T(8,128)(2,1)S(1)} %bitcast.8), channel_id=1, source_target_pairs={{0,112},{16,0},{32,16},{48,32},{64,48},{80,64},{96,80},{112,96},{1... | collective-permute-start | bytes 1572872 | tf_op jit(solution)/shard_map/ppermute | solution.py:101
  82.5 8.9 %collective-permute-done.5.refs_7_ = bf16[4,256,256]{2,1,0:T(8,128)(2,1)S(1)} collective-permute-done((bf16[4,256,256]{2,1,0:T(8,128)(2,1)S(1)}, bf16[4,256,256]{2,1,0:T(8,128)(2,1)S(1)}, u32[]{:S(2)}, u32[]{:S(2)}) %collective-permute-start.5) | collective-permute-done | bytes 524320 | tf_op jit(solution)/shard_map/ppermute | solution.py:100
  91.4 1.9 %collective-permute-start.6 = (bf16[4,256,256]{2,1,0:T(8,128)(2,1)S(1)}, bf16[4,256,256]{2,1,0:T(8,128)(2,1)S(1)}, u32[]{:S(2)}, u32[]{:S(2)}) collective-permute-start(bf16[4,256,256]{2,1,0:T(8,128)(2,1)S(1)} %collective-permute-done.5.refs_7_), channel_id=1, source_target_pairs={{0,16},{16,32},{32,48},{48,64},{64,80},{80,96},{96,112},{112,0},{1... | collective-permute-start | bytes 1572872 | tf_op jit(solution)/shard_map/ppermute | solution.py:100
  93.4 0.0 collective-permute-done.2.refs_1_
  93.4 5.1 %collective-permute-start.3 = (bf16[4,256,256]{2,1,0:T(8,128)(2,1)S(1)}, bf16[4,256,256]{2,1,0:T(8,128)(2,1)}, u32[]{:S(2)}, u32[]{:S(2)}) collective-permute-start(bf16[4,256,256]{2,1,0:T(8,128)(2,1)S(1)} %collective-permute-done.2.refs_1_), channel_id=1, source_target_pairs={{0,112},{16,0},{32,16},{48,32},{64,48},{80,64},{96,80},{112,96},{1... | collective-permute-start | bytes 1572872 | tf_op jit(solution)/shard_map/ppermute | solution.py:101
  98.5 8.0 %collective-permute-done.6.refs_6_ = bf16[4,256,256]{2,1,0:T(8,128)(2,1)S(1)} collective-permute-done((bf16[4,256,256]{2,1,0:T(8,128)(2,1)S(1)}, bf16[4,256,256]{2,1,0:T(8,128)(2,1)S(1)}, u32[]{:S(2)}, u32[]{:S(2)}) %collective-permute-start.6) | collective-permute-done | bytes 524320 | tf_op jit(solution)/shard_map/ppermute | solution.py:100
  106.5 1.9 %collective-permute-start.7 = (bf16[4,256,256]{2,1,0:T(8,128)(2,1)S(1)}, bf16[4,256,256]{2,1,0:T(8,128)(2,1)S(1)}, u32[]{:S(2)}, u32[]{:S(2)}) collective-permute-start(bf16[4,256,256]{2,1,0:T(8,128)(2,1)S(1)} %collective-permute-done.6.refs_6_), channel_id=1, source_target_pairs={{0,16},{16,32},{32,48},{48,64},{64,80},{80,96},{96,112},{112,0},{1... | collective-permute-start | bytes 1572872 | tf_op jit(solution)/shard_map/ppermute | solution.py:100
  108.4 0.0 collective-permute-done.3.refs_2_
  108.4 5.1 %collective-permute-start.4 = (bf16[4,256,256]{2,1,0:T(8,128)(2,1)}, bf16[4,256,256]{2,1,0:T(8,128)(2,1)S(1)}, u32[]{:S(2)}, u32[]{:S(2)}) collective-permute-start(bf16[4,256,256]{2,1,0:T(8,128)(2,1)} %collective-permute-done.3.refs_2_), channel_id=1, source_target_pairs={{0,112},{16,0},{32,16},{48,32},{64,48},{80,64},{96,80},{112,96},{1... | collective-permute-start | bytes 1572872 | tf_op jit(solution)/shard_map/ppermute | solution.py:101
  113.6 7.0 %collective-permute-done.7.refs_5_ = bf16[4,256,256]{2,1,0:T(8,128)(2,1)S(1)} collective-permute-done((bf16[4,256,256]{2,1,0:T(8,128)(2,1)S(1)}, bf16[4,256,256]{2,1,0:T(8,128)(2,1)S(1)}, u32[]{:S(2)}, u32[]{:S(2)}) %collective-permute-start.7) | collective-permute-done | bytes 524320 | tf_op jit(solution)/shard_map/ppermute | solution.py:100
  120.6 1.5 collective-permute-done.4.refs_3_
  122.1 0.8 broadcast_select_fusion
  123.0 1.9 %collective-permute-start.8 = (bf16[4,256,256]{2,1,0:T(8,128)(2,1)}, bf16[4,256,256]{2,1,0:T(8,128)(2,1)}, u32[]{:S(2)}, u32[]{:S(2)}) collective-permute-start(bf16[4,256,256]{2,1,0:T(8,128)(2,1)} %broadcast_select_fusion), channel_id=1, source_target_pairs={{0,16},{1,113},{2,18},{3,115},{4,20},{5,117},{6,22},{7,119},{8,24}... | collective-permute-start | bytes 1572872 | tf_op jit(solution)/shard_map/ppermute | solution.py:22
  124.9 0.1 pad_add_fusion.where
  125.0 11.0 %collective-permute-done.8.refs_4_ = bf16[4,256,256]{2,1,0:T(8,128)(2,1)} collective-permute-done((bf16[4,256,256]{2,1,0:T(8,128)(2,1)}, bf16[4,256,256]{2,1,0:T(8,128)(2,1)}, u32[]{:S(2)}, u32[]{:S(2)}) %collective-permute-start.8) | collective-permute-done | bytes 524320 | tf_op jit(solution)/shard_map/ppermute | solution.py:22
  135.9 0.0 all-gather.4.cloned.1.call-done
  135.9 0.0 all-gather.6.cloned.1.call-done
  135.9 9.1 %shard_map.37 = bf16[924,512]{1,0:T(8,128)(2,1)} custom-call(s32[3]{0:T(128)S(1)} %pad_add_fusion.where, bf16[924,2048]{1,0:T(8,128)(2,1)} %bitcast.10, bf16[924,2048]{1,0:T(8,128)(2,1)} %bitcast.11, bf16[4,256,256]{2,1,0:T(8,128)(2,1)S(1)} %bitcast.9, bf16[4,256,256]{2,1,0:T(8,128)(2,1)S(1)} %collective-permute-done.2.refs_1_, ...), custom_call_target="tpu_custom_call" | custom-call | flops 3875536896 | bytes 12582912 | tf_op jit(solution)/shard_map/pallas_call | solution.py:65
  (1 shorter events, 0.0 us)
Async XLA Ops:
  6.5 129.4 %all-gather.4.cloned.1.call-start = ((), (), s32[]{:S(2)}) async-start(), calls=%async_computation | async-start | bytes 4276224 | tf_op jit(solution)/shard_map/all_gather | solution.py:92
  7.3 128.7 %all-gather.6.cloned.1.call-start = ((), (), s32[]{:S(2)}) async-start(), calls=%async_computation.1 | async-start | bytes 4276224 | tf_op jit(solution)/shard_map/all_gather | solution.py:93
  7.3 25.8 %collective-permute-start = (bf16[256,924]{0,1:T(8,128)(2,1)}, bf16[256,924]{0,1:T(8,128)(2,1)S(1)}, u32[]{:S(2)}, u32[]{:S(2)}) collective-permute-start(bf16[256,924]{0,1:T(8,128)(2,1)} %param.3), channel_id=1, source_target_pairs={{0,2},{2,0},{1,3},{3,1},{4,6},{6,4},{5,7},{7,5},{8,10},{10,8},{9,1... | collective-permute-start | bytes 1419272 | tf_op jit(solution)/shard_map/ppermute | solution.py:91
  33.1 0.8 copy-start
  36.9 9.0 %collective-permute-start.1 = (bf16[256,256]{1,0:T(8,128)(2,1)S(1)}, bf16[256,256]{1,0:T(8,128)(2,1)S(1)}, u32[]{:S(2)}, u32[]{:S(2)}) collective-permute-start(bf16[256,256]{1,0:T(8,128)(2,1)S(1)} %broadcast_select_fusion.1), channel_id=1, source_target_pairs={{0,0},{1,8},{2,16},{3,24},{4,4},{5,12},{6,20},{7,28},{8,1},{9,9},{... | collective-permute-start | bytes 393224 | tf_op jit(solution)/shard_map/ppermute | solution.py:22
  65.3 26.1 %collective-permute-start.5 = (bf16[4,256,256]{2,1,0:T(8,128)(2,1)S(1)}, bf16[4,256,256]{2,1,0:T(8,128)(2,1)S(1)}, u32[]{:S(2)}, u32[]{:S(2)}) collective-permute-start(bf16[4,256,256]{2,1,0:T(8,128)(2,1)S(1)} %bitcast.7), channel_id=1, source_target_pairs={{0,16},{16,32},{32,48},{48,64},{64,80},{80,96},{96,112},{112,0},{1... | collective-permute-start | bytes 1572872 | tf_op jit(solution)/shard_map/ppermute | solution.py:100
  71.6 21.7 %collective-permute-start.2 = (bf16[4,256,256]{2,1,0:T(8,128)(2,1)S(1)}, bf16[4,256,256]{2,1,0:T(8,128)(2,1)S(1)}, u32[]{:S(2)}, u32[]{:S(2)}) collective-permute-start(bf16[4,256,256]{2,1,0:T(8,128)(2,1)S(1)} %bitcast.8), channel_id=1, source_target_pairs={{0,112},{16,0},{32,16},{48,32},{64,48},{80,64},{96,80},{112,96},{1... | collective-permute-start | bytes 1572872 | tf_op jit(solution)/shard_map/ppermute | solution.py:101
  91.4 15.0 %collective-permute-start.6 = (bf16[4,256,256]{2,1,0:T(8,128)(2,1)S(1)}, bf16[4,256,256]{2,1,0:T(8,128)(2,1)S(1)}, u32[]{:S(2)}, u32[]{:S(2)}) collective-permute-start(bf16[4,256,256]{2,1,0:T(8,128)(2,1)S(1)} %collective-permute-done.5.refs_7_), channel_id=1, source_target_pairs={{0,16},{16,32},{32,48},{48,64},{64,80},{80,96},{96,112},{112,0},{1... | collective-permute-start | bytes 1572872 | tf_op jit(solution)/shard_map/ppermute | solution.py:100
  93.4 15.0 %collective-permute-start.3 = (bf16[4,256,256]{2,1,0:T(8,128)(2,1)S(1)}, bf16[4,256,256]{2,1,0:T(8,128)(2,1)}, u32[]{:S(2)}, u32[]{:S(2)}) collective-permute-start(bf16[4,256,256]{2,1,0:T(8,128)(2,1)S(1)} %collective-permute-done.2.refs_1_), channel_id=1, source_target_pairs={{0,112},{16,0},{32,16},{48,32},{64,48},{80,64},{96,80},{112,96},{1... | collective-permute-start | bytes 1572872 | tf_op jit(solution)/shard_map/ppermute | solution.py:101
  106.5 14.1 %collective-permute-start.7 = (bf16[4,256,256]{2,1,0:T(8,128)(2,1)S(1)}, bf16[4,256,256]{2,1,0:T(8,128)(2,1)S(1)}, u32[]{:S(2)}, u32[]{:S(2)}) collective-permute-start(bf16[4,256,256]{2,1,0:T(8,128)(2,1)S(1)} %collective-permute-done.6.refs_6_), channel_id=1, source_target_pairs={{0,16},{16,32},{32,48},{48,64},{64,80},{80,96},{96,112},{112,0},{1... | collective-permute-start | bytes 1572872 | tf_op jit(solution)/shard_map/ppermute | solution.py:100
  108.4 13.7 %collective-permute-start.4 = (bf16[4,256,256]{2,1,0:T(8,128)(2,1)}, bf16[4,256,256]{2,1,0:T(8,128)(2,1)S(1)}, u32[]{:S(2)}, u32[]{:S(2)}) collective-permute-start(bf16[4,256,256]{2,1,0:T(8,128)(2,1)} %collective-permute-done.3.refs_2_), channel_id=1, source_target_pairs={{0,112},{16,0},{32,16},{48,32},{64,48},{80,64},{96,80},{112,96},{1... | collective-permute-start | bytes 1572872 | tf_op jit(solution)/shard_map/ppermute | solution.py:101
  123.0 13.0 %collective-permute-start.8 = (bf16[4,256,256]{2,1,0:T(8,128)(2,1)}, bf16[4,256,256]{2,1,0:T(8,128)(2,1)}, u32[]{:S(2)}, u32[]{:S(2)}) collective-permute-start(bf16[4,256,256]{2,1,0:T(8,128)(2,1)} %broadcast_select_fusion), channel_id=1, source_target_pairs={{0,16},{1,113},{2,18},{3,115},{4,20},{5,117},{6,22},{7,119},{8,24}... | collective-permute-start | bytes 1572872 | tf_op jit(solution)/shard_map/ppermute | solution.py:22
Sparse Core Ops, SparseCore 0:
  9.5 43.7 all-gather.3
  55.4 43.5 all-gather.5

commit v2 on v0

v2 whole, which is shorter than its diff:
```python
import itertools

import jax
import jax.numpy as jnp
from jax import lax
from jax.experimental import pallas as pl
from jax.experimental.pallas import tpu as pltpu
from jax.sharding import Mesh, PartitionSpec as P

ROWBLK = 128
MROWS = 256
VMEM = 56 << 20
NX, NZ, NYL, NYH, NC = 4, 8, 4, 2, 2
ALL = ("x", "z", "yl", "yh", "c")
PLACES = list(itertools.product(range(NX), range(NZ), range(NYL), range(NYH), range(NC)))


def linear(x, z, yl, yh, c):
    return (((x * NZ + z) * NYL + yl) * NYH + yh) * NC + c


def permute(value, target):
    return lax.ppermute(value, ALL, [(linear(*p), linear(*target(*p))) for p in PLACES])


def to_owner_plane(x, z, yl, yh, c):
    return z // 2, z ^ (2 * x + yh), 2 * c + yl % 2, z % 2, yl // 2


def other_half(x, z, yl, yh, c):
    return x, z, yl, 1 - yh, c


def other_core(x, z, yl, yh, c):
    return x, z, yl, yh, 1 - c


def product(place, counts, stashes, grads, width):
    rows, cols, pad = 2 * MROWS, 2 * MROWS, stashes[0].shape[1]

    def kernel(place_ref, counts_ref, *refs):
        s_refs, (g_ref, out_ref, s_vm, g_vm, total, s_sem, g_sem) = refs[:4], refs[4:]
        x0, yh0, c0 = (place_ref[i] for i in range(3))
        own = 2 * x0 + yh0

        def stash_copies(x, h):
            q = 2 * x + (yh0 if h == 0 else 1 - yh0)
            return [
                pltpu.make_async_copy(
                    s_refs[2 * h + i].at[x],
                    s_vm.at[q, :, pl.ds(pl.multiple_of((c0 if i == 0 else 1 - c0) * MROWS, MROWS), MROWS)],
                    s_sem.at[q],
                )
                for i in range(NC)
            ]

        def grad_copies(q):
            return [
                pltpu.make_async_copy(
                    g_ref.at[q ^ own, b],
                    g_vm.at[q, pl.ds((b // 2) * MROWS, MROWS), pl.ds((b % 2) * MROWS, MROWS)],
                    g_sem.at[q],
                )
                for b in range(NYL)
            ]

        for q in range(NZ):
            for copy in grad_copies(q):
                copy.start()
            for copy in stash_copies(q // 2, q % 2):
                copy.start()
        for x in range(NX):
            for h in range(NYH):
                for copy in stash_copies(x, h):
                    copy.wait()
        for q in range(NZ):
            for copy in grad_copies(q):
                copy.wait()
            for c in range(NC):
                @pl.when(counts_ref[2 * q + c] < 2)
                def _():
                    g_vm[q, pl.ds(c * MROWS + ROWBLK, ROWBLK), :] = jnp.zeros((ROWBLK, cols), jnp.bfloat16)
            part = jnp.dot(s_vm[q], g_vm[q], preferred_element_type=jnp.float32)
            if q == 0:
                total[...] = part
            elif q < NZ - 1:
                total[...] += part
            else:
                out_ref[...] = (total[...] + part)[:width].astype(jnp.bfloat16)

    return pl.pallas_call(
        kernel,
        out_shape=jax.ShapeDtypeStruct((width, cols), jnp.bfloat16),
        in_specs=[pl.BlockSpec(memory_space=pltpu.SMEM)] * 2 + [pl.BlockSpec(memory_space=pl.ANY)] * 5,
        out_specs=pl.BlockSpec(memory_space=pltpu.VMEM),
        scratch_shapes=[
            pltpu.VMEM((NZ, pad, rows), jnp.bfloat16),
            pltpu.VMEM((NZ, rows, cols), jnp.bfloat16),
            pltpu.VMEM((pad, cols), jnp.float32),
            pltpu.SemaphoreType.DMA((NZ,)),
            pltpu.SemaphoreType.DMA((NZ,)),
        ],
        compiler_params=pltpu.CompilerParams(vmem_limit_bytes=VMEM),
        cost_estimate=pl.CostEstimate(flops=16 * pad * rows * cols, bytes_accessed=13 << 20, transcendentals=0),
    )(place, counts, *stashes, grads)


def together(*values):
    return lax.optimization_barrier(values)


def spread(block, axis, size):
    return lax.all_to_all(jnp.broadcast_to(block, (size, *block.shape)), axis, 0, 0)


def shards(stash, out_grads, block_counts):
    place = jnp.stack([lax.axis_index(a) for a in ("x", "yh", "c")]).astype(jnp.int32)
    width = stash.shape[1]
    own = jnp.pad(stash.T, ((0, -width % 32), (0, 0)))

    near = permute(out_grads, to_owner_plane)
    piece = lax.all_gather(near, "yl", axis=0, tiled=True)
    grads = lax.all_gather(piece, "z", axis=0, tiled=True)

    piece, own = together(piece, own)
    partner = permute(own, other_half)
    own4 = spread(own, "x", NX)
    partner4 = spread(partner, "x", NX)
    stashes = [own4, permute(own4, other_core), partner4, permute(partner4, other_core)]
    return product(place, block_counts, stashes, grads.reshape(NZ, NYL, MROWS, MROWS), width)


def solution(mesh):
    fine = Mesh(mesh.devices.reshape(NX, NZ, NYL, NYH, NC), ALL)
    rows, features = ("x", "yh", "c"), ("z", "yl")
    placed = (P(rows, features), P(rows, features), P())
    return jax.shard_map(shards, mesh=fine, in_specs=placed, out_specs=P(features, rows), check_vma=False)
```

time: 372 us -> 129 us (0.35)
  the two profiles are of different devices: /device:TPU:49 before, /device:TPU:193 now
where the time goes in v2:
time: 129 us
  waiting for transfers between devices  52.1 us (40%)
  starting transfers between devices  32 us (25%)
  blocking collectives  16.1 us (12%)
  between operations  13.5 us (10%)
  Pallas kernels  10.7 us (8%)
  local copies, waits for them, and re-layouts  3.94 us (3%)
    ppermute x4, waiting for transfers between devices, permute(): lax.ppermute(value, ALL, [(linear(*p), linear(*target(*p))) for p in PLAC...  33.2 us
    ppermute x4, starting transfers between devices, permute(): lax.ppermute(value, ALL, [(linear(*p), linear(*target(*p))) for p in PLAC...  19.8 us
    all_to_all x2, waiting for transfers between devices, spread(): lax.all_to_all(jnp.broadcast_to(block, (size, *block.shape)), axis, 0, 0)  18.9 us
    all_gather x1, blocking collectives, shards(): piece = lax.all_gather(near, 'yl', axis=0, tiled=True)  16.1 us
    all_to_all x2, starting transfers between devices, spread(): lax.all_to_all(jnp.broadcast_to(block, (size, *block.shape)), axis, 0, 0)  12.2 us
    pallas_call x1, Pallas kernels, product(): pl.pallas_call(kernel, out_shape=jax.ShapeDtypeStruct((width, cols), jnp....  10.7 us
    broadcast_in_dim x2, local copies, waits for them, and re-layouts, spread(): jnp.broadcast_to(block, (size, *block.shape))  2.87 us
  transfers between devices with their start and end apart: 7, of which 4 were waited for; matrix products, arithmetic and copies ran while one was open for 4% of the time, Pallas kernels for 0%

profile of v2, /device:TPU:193, one launch (start us, length us, event | category | flops | bytes accessed | tf_op | source)
XLA Modules:
  0.0 128.9 jit_solution(8127686911352192997)
XLA Ops:
  6.5 0.0 all-gather.2.cloned.1.call-start
  6.5 7.4 %collective-permute-start = (bf16[256,256]{1,0:T(8,128)(2,1)}, bf16[256,256]{1,0:T(8,128)(2,1)S(1)}, u32[]{:S(2)}, u32[]{:S(2)}) collective-permute-start(bf16[256,256]{1,0:T(8,128)(2,1)} %param.4), channel_id=1, source_target_pairs={{0,0},{1,8},{2,16},{3,24},{4,4},{5,12},{6,20},{7,28},{8,1},{9,9},{... | collective-permute-start | bytes 393224 | tf_op jit(solution)/shard_map/ppermute | solution.py:23
  13.9 6.5 %collective-permute-done = bf16[256,256]{1,0:T(8,128)(2,1)S(1)} collective-permute-done((bf16[256,256]{1,0:T(8,128)(2,1)}, bf16[256,256]{1,0:T(8,128)(2,1)S(1)}, u32[]{:S(2)}, u32[]{:S(2)}) %collective-permute-start) | collective-permute-done | bytes 131104 | tf_op jit(solution)/shard_map/ppermute | solution.py:23
  20.4 16.1 %all_gather.6 = bf16[1024,256]{1,0:T(8,128)(2,1)} all-gather(bf16[256,256]{1,0:T(8,128)(2,1)S(1)} %collective-permute-done), channel_id=1, replica_groups=mesh['x'=4,'z'=8,'yl'=4,'yh'=2,'c'=2] {'yl'}, dimensions={0}, use_global_device_ids=true | all-gather | bytes 655360 | tf_op jit(solution)/shard_map/all_gather | solution.py:122
  36.4 0.0 all-gather.2.cloned.1.call-update
  36.4 1.1 pad.4
  37.5 1.4 %broadcast_in_dim.6 = bf16[4,928,256]{2,1,0:T(8,128)(2,1)} broadcast(bf16[928,256]{1,0:T(8,128)(2,1)S(1)} %pad.4), dimensions={1,2} | broadcast | bytes 2375680 | tf_op jit(solution)/shard_map/broadcast_in_dim | solution.py:113
  38.9 7.8 %all-to-all-start = ((bf16[4,928,256]{2,1,0:T(8,128)(2,1)}), bf16[4,928,256]{2,1,0:T(8,128)(2,1)S(1)}, u32[]{:S(2)}, u32[]{:S(2)}) async-start(bf16[4,928,256]{2,1,0:T(8,128)(2,1)} %broadcast_in_dim.6), calls=%async_computation | async-start | bytes 3801088 | tf_op jit(solution)/shard_map/all_to_all | solution.py:113
  46.7 4.3 %collective-permute-start.2 = (bf16[928,256]{1,0:T(8,128)(2,1)S(1)}, bf16[928,256]{1,0:T(8,128)(2,1)S(1)}, u32[]{:S(2)}, u32[]{:S(2)}) collective-permute-start(bf16[928,256]{1,0:T(8,128)(2,1)S(1)} %pad.4), channel_id=1, source_target_pairs={{0,2},{1,3},{2,0},{3,1},{4,6},{5,7},{6,4},{7,5},{8,10},{9,11},{10,... | collective-permute-start | bytes 1425416 | tf_op jit(solution)/shard_map/ppermute | solution.py:23
  51.0 23.5 %collective-permute-done.2 = bf16[928,256]{1,0:T(8,128)(2,1)S(1)} collective-permute-done((bf16[928,256]{1,0:T(8,128)(2,1)S(1)}, bf16[928,256]{1,0:T(8,128)(2,1)S(1)}, u32[]{:S(2)}, u32[]{:S(2)}) %collective-permute-start.2) | collective-permute-done | bytes 475168 | tf_op jit(solution)/shard_map/ppermute | solution.py:23
  74.4 0.0 all-to-all-done.refs_0_
  74.5 0.0 copy-start
  74.5 1.5 %broadcast_in_dim.7 = bf16[4,928,256]{2,1,0:T(8,128)(2,1)} broadcast(bf16[928,256]{1,0:T(8,128)(2,1)S(1)} %collective-permute-done.2), dimensions={1,2} | broadcast | bytes 2375680 | tf_op jit(solution)/shard_map/broadcast_in_dim | solution.py:113
  75.9 4.4 %all-to-all-start.1 = ((bf16[4,928,256]{2,1,0:T(8,128)(2,1)}), bf16[4,928,256]{2,1,0:T(8,128)(2,1)}, u32[]{:S(2)}, u32[]{:S(2)}) async-start(bf16[4,928,256]{2,1,0:T(8,128)(2,1)} %broadcast_in_dim.7), calls=%async_computation.1 | async-start | bytes 3801088 | tf_op jit(solution)/shard_map/all_to_all | solution.py:113
  80.4 0.0 copy-done
  80.4 3.6 %collective-permute-start.1 = (bf16[4,928,256]{2,1,0:T(8,128)(2,1)S(1)}, bf16[4,928,256]{2,1,0:T(8,128)(2,1)}, u32[]{:S(2)}, u32[]{:S(2)}) collective-permute-start(bf16[4,928,256]{2,1,0:T(8,128)(2,1)S(1)} %all-to-all-done.refs_0_), channel_id=1, source_target_pairs={{0,1},{1,0},{2,3},{3,2},{4,5},{5,4},{6,7},{7,6},{8,9},{9,8},{10,11... | collective-permute-start | bytes 5701640 | tf_op jit(solution)/shard_map/ppermute | solution.py:23
  84.0 18.9 %all-to-all-done.1.refs_2_ = bf16[4,928,256]{2,1,0:T(8,128)(2,1)} async-done(((bf16[4,928,256]{2,1,0:T(8,128)(2,1)}), bf16[4,928,256]{2,1,0:T(8,128)(2,1)}, u32[]{:S(2)}, u32[]{:S(2)}) %all-to-all-start.1) | async-done | bytes 1900576 | tf_op jit(solution)/shard_map/all_to_all | solution.py:113
  102.9 4.6 %collective-permute-start.3 = (bf16[4,928,256]{2,1,0:T(8,128)(2,1)}, bf16[4,928,256]{2,1,0:T(8,128)(2,1)}, u32[]{:S(2)}, u32[]{:S(2)}) collective-permute-start(bf16[4,928,256]{2,1,0:T(8,128)(2,1)} %all-to-all-done.1.refs_2_), channel_id=1, source_target_pairs={{0,1},{1,0},{2,3},{3,2},{4,5},{5,4},{6,7},{7,6},{8,9},{9,8},{10,11... | collective-permute-start | bytes 5701640 | tf_op jit(solution)/shard_map/ppermute | solution.py:23
  107.5 0.6 pad_add_fusion.place_ref
  108.1 0.0 collective-permute-done.1.refs_1_
  108.1 3.2 %collective-permute-done.3.refs_3_ = bf16[4,928,256]{2,1,0:T(8,128)(2,1)} collective-permute-done((bf16[4,928,256]{2,1,0:T(8,128)(2,1)}, bf16[4,928,256]{2,1,0:T(8,128)(2,1)}, u32[]{:S(2)}, u32[]{:S(2)}) %collective-permute-start.3) | collective-permute-done | bytes 1900576 | tf_op jit(solution)/shard_map/ppermute | solution.py:23
  111.3 0.0 all-gather.2.cloned.1.call-done
  111.3 10.7 %shard_map.37 = bf16[924,512]{1,0:T(8,128)(2,1)} custom-call(s32[3]{0:T(128)} %pad_add_fusion.place_ref, s32[16]{0:T(128)} %counts_ref.1, bf16[4,928,256]{2,1,0:T(8,128)(2,1)} %copy-done, bf16[4,928,256]{2,1,0:T(8,128)(2,1)} %collective-permute-done.1.refs_1_, bf16[4,928,256]{2,1,0:T(8,128)(2,1)} %all-to-all-done.1.refs_2_, ...), custom_call_target="tpu_custom_call" | custom-call | flops 3892314112 | bytes 13631488 | tf_op jit(solution)/shard_map/pallas_call | solution.py:91
Async XLA Ops:
  6.5 104.8 %all-gather.2.cloned.1.call-start = ((), (), s32[]{:S(2)}) async-start(), calls=%async_computation.2 | async-start | bytes 4718592 | tf_op jit(solution)/shard_map/all_gather | solution.py:123
  6.5 13.8 %collective-permute-start = (bf16[256,256]{1,0:T(8,128)(2,1)}, bf16[256,256]{1,0:T(8,128)(2,1)S(1)}, u32[]{:S(2)}, u32[]{:S(2)}) collective-permute-start(bf16[256,256]{1,0:T(8,128)(2,1)} %param.4), channel_id=1, source_target_pairs={{0,0},{1,8},{2,16},{3,24},{4,4},{5,12},{6,20},{7,28},{8,1},{9,9},{... | collective-permute-start | bytes 393224 | tf_op jit(solution)/shard_map/ppermute | solution.py:23
  38.9 35.5 %all-to-all-start = ((bf16[4,928,256]{2,1,0:T(8,128)(2,1)}), bf16[4,928,256]{2,1,0:T(8,128)(2,1)S(1)}, u32[]{:S(2)}, u32[]{:S(2)}) async-start(bf16[4,928,256]{2,1,0:T(8,128)(2,1)} %broadcast_in_dim.6), calls=%async_computation | async-start | bytes 3801088 | tf_op jit(solution)/shard_map/all_to_all | solution.py:113
  46.7 27.7 %collective-permute-start.2 = (bf16[928,256]{1,0:T(8,128)(2,1)S(1)}, bf16[928,256]{1,0:T(8,128)(2,1)S(1)}, u32[]{:S(2)}, u32[]{:S(2)}) collective-permute-start(bf16[928,256]{1,0:T(8,128)(2,1)S(1)} %pad.4), channel_id=1, source_target_pairs={{0,2},{1,3},{2,0},{3,1},{4,6},{5,7},{6,4},{7,5},{8,10},{9,11},{10,... | collective-permute-start | bytes 1425416 | tf_op jit(solution)/shard_map/ppermute | solution.py:23
  74.5 5.9 %copy-start = (bf16[4,928,256]{2,1,0:T(8,128)(2,1)}, bf16[4,928,256]{2,1,0:T(8,128)(2,1)S(1)}, u32[]{:S(2)}) copy-start(bf16[4,928,256]{2,1,0:T(8,128)(2,1)S(1)} %all-to-all-done.refs_0_) | copy-start | bytes 5701636
  75.9 27.0 %all-to-all-start.1 = ((bf16[4,928,256]{2,1,0:T(8,128)(2,1)}), bf16[4,928,256]{2,1,0:T(8,128)(2,1)}, u32[]{:S(2)}, u32[]{:S(2)}) async-start(bf16[4,928,256]{2,1,0:T(8,128)(2,1)} %broadcast_in_dim.7), calls=%async_computation.1 | async-start | bytes 3801088 | tf_op jit(solution)/shard_map/all_to_all | solution.py:113
  80.4 27.7 %collective-permute-start.1 = (bf16[4,928,256]{2,1,0:T(8,128)(2,1)S(1)}, bf16[4,928,256]{2,1,0:T(8,128)(2,1)}, u32[]{:S(2)}, u32[]{:S(2)}) collective-permute-start(bf16[4,928,256]{2,1,0:T(8,128)(2,1)S(1)} %all-to-all-done.refs_0_), channel_id=1, source_target_pairs={{0,1},{1,0},{2,3},{3,2},{4,5},{5,4},{6,7},{7,6},{8,9},{9,8},{10,11... | collective-permute-start | bytes 5701640 | tf_op jit(solution)/shard_map/ppermute | solution.py:23
  102.9 8.4 %collective-permute-start.3 = (bf16[4,928,256]{2,1,0:T(8,128)(2,1)}, bf16[4,928,256]{2,1,0:T(8,128)(2,1)}, u32[]{:S(2)}, u32[]{:S(2)}) collective-permute-start(bf16[4,928,256]{2,1,0:T(8,128)(2,1)} %all-to-all-done.1.refs_2_), channel_id=1, source_target_pairs={{0,1},{1,0},{2,3},{3,2},{4,5},{5,4},{6,7},{7,6},{8,9},{9,8},{10,11... | collective-permute-start | bytes 5701640 | tf_op jit(solution)/shard_map/ppermute | solution.py:23
Sparse Core Ops, SparseCore 0:
  36.6 62.1 all-gather.1

commit v3 on v2

v3 whole, which is shorter than its diff:
```python
import itertools

import jax
import jax.numpy as jnp
from jax import lax
from jax.experimental import pallas as pl
from jax.experimental.pallas import tpu as pltpu
from jax.sharding import Mesh, PartitionSpec as P

ROWBLK = 128
MROWS = 256
VMEM = 60 << 20
NX, NZ, NYL, NYH, NC = 4, 8, 4, 2, 2
ALL = ("x", "z", "yl", "yh", "c")
PLACES = list(itertools.product(range(NX), range(NZ), range(NYL), range(NYH), range(NC)))


def linear(x, z, yl, yh, c):
    return (((x * NZ + z) * NYL + yl) * NYH + yh) * NC + c


def permute(value, target):
    return lax.ppermute(value, ALL, [(linear(*p), linear(*target(*p))) for p in PLACES])


def to_owner_plane(x, z, yl, yh, c):
    return z // 2, z ^ (2 * x + yh), 2 * c + yl % 2, z % 2, yl // 2


def other_half(x, z, yl, yh, c):
    return x, z, yl, 1 - yh, c


def other_core(x, z, yl, yh, c):
    return x, z, yl, yh, 1 - c


def along_x(steps):
    return lambda x, z, yl, yh, c: ((x + steps) % NX, z, yl, yh, c)


def product(place, counts, stashes, grads, width):
    rows, cols = 2 * MROWS, 2 * MROWS
    arrays = []
    for _, *sides in stashes:
        for _, array in sides:
            if not any(array is a for a in arrays):
                arrays.append(array)
    where_is = [[(i, [array is a for a in arrays].index(True)) for i, array in sides] for _, *sides in stashes]
    keys = [key for key, *_ in stashes]
    pad, ns, ng = arrays[0].shape[-2], len(arrays), len(grads)

    def kernel(place_ref, counts_ref, *refs):
        s_refs, g_refs, (out_ref, s_vm, g_vm, total, s_sem, g_sem) = refs[:ns], refs[ns : ns + ng], refs[ns + ng :]
        x0, z0, yh0, c0 = (place_ref[i] for i in range(4))
        own = 2 * x0 + yh0

        def q_of(j):
            h, back = keys[j]
            return 2 * lax.rem(x0 - back + NX, NX) + (yh0 if h == 0 else 1 - yh0)

        def grad_copies(j, ref):
            return [
                pltpu.make_async_copy(
                    ref.at[b],
                    g_vm.at[j, pl.ds((b // 2) * MROWS, MROWS), pl.ds((b % 2) * MROWS, MROWS)],
                    g_sem.at[j],
                )
                for b in range(NYL)
            ]

        for j in range(len(keys)):
            if ng == 1:
                for copy in grad_copies(j, g_refs[0].at[q_of(j) ^ own]):
                    copy.start()
            else:
                for d in range(NZ):
                    @pl.when((q_of(j) ^ own) == lax.rem(z0 - d * (1 - 2 * c0) + NZ, NZ))
                    def _():
                        for copy in grad_copies(j, g_refs[d]):
                            copy.start()
            for side, (i, n) in enumerate(where_is[j]):
                c = c0 if side == 0 else 1 - c0
                at = s_vm.at[j, :, pl.ds(pl.multiple_of(c * MROWS, MROWS), MROWS)]
                pltpu.make_async_copy(s_refs[n] if i is None else s_refs[n].at[i], at, s_sem.at[j]).start()
        for j in range(len(keys)):
            for copy in grad_copies(j, g_refs[0].at[0] if ng == 1 else g_refs[0]):
                copy.wait()
            for c in range(NC):
                @pl.when(counts_ref[2 * q_of(j) + c] < 2)
                def _():
                    g_vm[j, pl.ds(c * MROWS + ROWBLK, ROWBLK), :] = jnp.zeros((ROWBLK, cols), jnp.bfloat16)
            for c in range(NC):
                at = s_vm.at[j, :, pl.ds(c * MROWS, MROWS)]
                pltpu.make_async_copy(at, at, s_sem.at[j]).wait()
            part = jnp.dot(s_vm[j], g_vm[j], preferred_element_type=jnp.float32)
            if j == 0:
                total[...] = part
            elif j < NZ - 1:
                total[...] += part
            else:
                out_ref[...] = (total[...] + part)[:width].astype(jnp.bfloat16)

    return pl.pallas_call(
        kernel,
        out_shape=jax.ShapeDtypeStruct((width, cols), jnp.bfloat16),
        in_specs=[pl.BlockSpec(memory_space=pltpu.SMEM)] * 2 + [pl.BlockSpec(memory_space=pl.ANY)] * (ns + ng),
        out_specs=pl.BlockSpec(memory_space=pltpu.VMEM),
        scratch_shapes=[
            pltpu.VMEM((NZ, pad, rows), jnp.bfloat16),
            pltpu.VMEM((NZ, rows, cols), jnp.bfloat16),
            pltpu.VMEM((pad, cols), jnp.float32),
            pltpu.SemaphoreType.DMA((NZ,)),
            pltpu.SemaphoreType.DMA((NZ,)),
        ],
        compiler_params=pltpu.CompilerParams(vmem_limit_bytes=VMEM),
        cost_estimate=pl.CostEstimate(flops=16 * pad * rows * cols, bytes_accessed=13 << 20, transcendentals=0),
    )(place, counts, *arrays, *grads)


def together(*values):
    return lax.optimization_barrier(values)


def shards(stash, out_grads, block_counts):
    place = jnp.stack([lax.axis_index(a) for a in ("x", "z", "yh", "c")]).astype(jnp.int32)
    width = stash.shape[1]
    own = jnp.pad(stash.T, ((0, -width % 32), (0, 0)))

    near = permute(out_grads, to_owner_plane)
    near, own = together(near, own)
    piece = lax.all_gather(near, "yl", axis=0, tiled=True)
    grads = [lax.all_gather(piece, "z", axis=0, tiled=True).reshape(NZ, NYL, MROWS, MROWS)]

    piece, own = together(piece, own)
    partner = permute(own, other_half)
    sides = []
    for h, block in enumerate((own, partner)):
        moved = [permute(block, along_x(back)) for back in (1, 3, 2)]
        backs = (0, 1, 3, 2)
        if h == 0:
            mine = jnp.stack([block, *moved])
            theirs = permute(mine, other_core)
            sides += [((h, back), (i, mine), (i, theirs)) for i, back in enumerate(backs)]
        else:
            mine = jnp.stack(moved)
            theirs = permute(mine, other_core)
            sides.append(((h, 0), (None, block), (None, permute(block, other_core))))
            sides += [((h, back), (i, mine), (i, theirs)) for i, back in enumerate(backs[1:])]
    return product(place, block_counts, sides, grads, width)


def solution(mesh):
    fine = Mesh(mesh.devices.reshape(NX, NZ, NYL, NYH, NC), ALL)
    rows, features = ("x", "yh", "c"), ("z", "yl")
    placed = (P(rows, features), P(rows, features), P())
    return jax.shard_map(shards, mesh=fine, in_specs=placed, out_specs=P(features, rows), check_vma=False)
```

time: 129 us -> 118 us (0.915)
  the two profiles are of different devices: /device:TPU:193 before, /device:TPU:1 now
where the time goes in v3:
time: 118 us
  starting transfers between devices  59.4 us (50%)
  waiting for transfers between devices  20 us (17%)
  blocking collectives  14.7 us (12%)
  between operations  13.6 us (12%)
  Pallas kernels  8.21 us (7%)
    ppermute x11, starting transfers between devices, permute(): lax.ppermute(value, ALL, [(linear(*p), linear(*target(*p))) for p in PLAC...  59.4 us
    ppermute x11, waiting for transfers between devices, permute(): lax.ppermute(value, ALL, [(linear(*p), linear(*target(*p))) for p in PLAC...  17.5 us
    all_gather x1, blocking collectives, shards(): piece = lax.all_gather(near, 'yl', axis=0, tiled=True)  14.7 us
    pallas_call x1, Pallas kernels, product(): pl.pallas_call(kernel, out_shape=jax.ShapeDtypeStruct((width, cols), jnp....  8.21 us
    all_gather x1, waiting for transfers between devices, shards(): lax.all_gather(piece, 'z', axis=0, tiled=True)  2.56 us
  transfers between devices with their start and end apart: 12, of which 6 were waited for; matrix products, arithmetic and copies ran while one was open for 2% of the time, Pallas kernels for 0%

profile of v3, /device:TPU:1, one launch (start us, length us, event | category | flops | bytes accessed | tf_op | source)
XLA Modules:
  0.0 118.0 jit_solution(2175508975810225532)
XLA Ops:
  6.5 0.0 all-gather.2.cloned.1.call-start
  6.5 5.6 %collective-permute-start = (bf16[256,256]{1,0:T(8,128)(2,1)}, bf16[256,256]{1,0:T(8,128)(2,1)S(1)}, u32[]{:S(2)}, u32[]{:S(2)}) collective-permute-start(bf16[256,256]{1,0:T(8,128)(2,1)} %param.4), channel_id=1, source_target_pairs={{0,0},{1,8},{2,16},{3,24},{4,4},{5,12},{6,20},{7,28},{8,1},{9,9},{... | collective-permute-start | bytes 393224 | tf_op jit(solution)/shard_map/ppermute | solution.py:23
  12.1 1.1 pad.4
  13.2 3.2 %collective-permute-done = bf16[256,256]{1,0:T(8,128)(2,1)S(1)} collective-permute-done((bf16[256,256]{1,0:T(8,128)(2,1)}, bf16[256,256]{1,0:T(8,128)(2,1)S(1)}, u32[]{:S(2)}, u32[]{:S(2)}) %collective-permute-start) | collective-permute-done | bytes 131104 | tf_op jit(solution)/shard_map/ppermute | solution.py:23
  16.4 14.7 %all_gather.6 = bf16[1024,256]{1,0:T(8,128)(2,1)} all-gather(bf16[256,256]{1,0:T(8,128)(2,1)S(1)} %collective-permute-done), channel_id=1, replica_groups=mesh['x'=4,'z'=8,'yl'=4,'yh'=2,'c'=2] {'yl'}, dimensions={0}, use_global_device_ids=true | all-gather | bytes 655360 | tf_op jit(solution)/shard_map/all_gather | solution.py:132
  31.1 0.0 all-gather.2.cloned.1.call-update
  31.1 8.6 %collective-permute-start.5 = (bf16[928,256]{1,0:T(8,128)(2,1)S(1)}, bf16[928,256]{1,0:T(8,128)(2,1)}, u32[]{:S(2)}, u32[]{:S(2)}) collective-permute-start(bf16[928,256]{1,0:T(8,128)(2,1)S(1)} %pad.4), channel_id=1, source_target_pairs={{0,2},{1,3},{2,0},{3,1},{4,6},{5,7},{6,4},{7,5},{8,10},{9,11},{10,... | collective-permute-start | bytes 1425416 | tf_op jit(solution)/shard_map/ppermute | solution.py:23
  39.7 11.7 %collective-permute-start.3 = (bf16[928,256]{1,0:T(8,128)(2,1)S(1)}, bf16[928,256]{1,0:T(8,128)(2,1)S(1)}, u32[]{:S(2)}, u32[]{:S(2)}) collective-permute-start(bf16[928,256]{1,0:T(8,128)(2,1)S(1)} %pad.4), channel_id=1, source_target_pairs={{0,256},{1,257},{2,258},{3,259},{4,260},{5,261},{6,262},{7,263},{8... | collective-permute-start | bytes 1425416 | tf_op jit(solution)/shard_map/ppermute | solution.py:23
  51.4 1.9 %collective-permute-start.2 = (bf16[928,256]{1,0:T(8,128)(2,1)S(1)}, bf16[928,256]{1,0:T(8,128)(2,1)S(1)}, u32[]{:S(2)}, u32[]{:S(2)}) collective-permute-start(bf16[928,256]{1,0:T(8,128)(2,1)S(1)} %pad.4), channel_id=1, source_target_pairs={{0,384},{1,385},{2,386},{3,387},{4,388},{5,389},{6,390},{7,391},{8... | collective-permute-start | bytes 1425416 | tf_op jit(solution)/shard_map/ppermute | solution.py:23
  53.4 3.4 %collective-permute-start.1 = (bf16[928,256]{1,0:T(8,128)(2,1)S(1)}, bf16[928,256]{1,0:T(8,128)(2,1)S(1)}, u32[]{:S(2)}, u32[]{:S(2)}) collective-permute-start(bf16[928,256]{1,0:T(8,128)(2,1)S(1)} %pad.4), channel_id=1, source_target_pairs={{0,128},{1,129},{2,130},{3,131},{4,132},{5,133},{6,134},{7,135},{8... | collective-permute-start | bytes 1425416 | tf_op jit(solution)/shard_map/ppermute | solution.py:23
  56.7 0.0 collective-permute-done.5.refs_2_
  56.7 7.8 %collective-permute-start.9 = (bf16[928,256]{1,0:T(8,128)(2,1)}, bf16[928,256]{1,0:T(8,128)(2,1)S(1)}, u32[]{:S(2)}, u32[]{:S(2)}) collective-permute-start(bf16[928,256]{1,0:T(8,128)(2,1)} %collective-permute-done.5.refs_2_), channel_id=1, source_target_pairs={{0,256},{1,257},{2,258},{3,259},{4,260},{5,261},{6,262},{7,263},{8... | collective-permute-start | bytes 1425416 | tf_op jit(solution)/shard_map/ppermute | solution.py:23
  64.6 8.7 %collective-permute-start.8 = (bf16[928,256]{1,0:T(8,128)(2,1)}, bf16[928,256]{1,0:T(8,128)(2,1)S(1)}, u32[]{:S(2)}, u32[]{:S(2)}) collective-permute-start(bf16[928,256]{1,0:T(8,128)(2,1)} %collective-permute-done.5.refs_2_), channel_id=1, source_target_pairs={{0,384},{1,385},{2,386},{3,387},{4,388},{5,389},{6,390},{7,391},{8... | collective-permute-start | bytes 1425416 | tf_op jit(solution)/shard_map/ppermute | solution.py:23
  73.3 0.0 collective-permute-done.3
  73.3 2.5 %collective-permute-start.7 = (bf16[928,256]{1,0:T(8,128)(2,1)}, bf16[928,256]{1,0:T(8,128)(2,1)S(1)}, u32[]{:S(2)}, u32[]{:S(2)}) collective-permute-start(bf16[928,256]{1,0:T(8,128)(2,1)} %collective-permute-done.5.refs_2_), channel_id=1, source_target_pairs={{0,128},{1,129},{2,130},{3,131},{4,132},{5,133},{6,134},{7,135},{8... | collective-permute-start | bytes 1425416 | tf_op jit(solution)/shard_map/ppermute | solution.py:23
  75.8 0.0 collective-permute-done.2
  75.8 0.0 collective-permute-done.1
  75.8 0.2 pad_maximum_fusion.refs_0_
  76.1 0.0 copy-start
  76.1 4.6 %collective-permute-start.4 = (bf16[4,928,256]{2,1,0:T(8,128)(2,1)S(1)}, bf16[4,928,256]{2,1,0:T(8,128)(2,1)}, u32[]{:S(2)}, u32[]{:S(2)}) collective-permute-start(bf16[4,928,256]{2,1,0:T(8,128)(2,1)S(1)} %pad_maximum_fusion.refs_0_), channel_id=1, source_target_pairs={{0,1},{1,0},{2,3},{3,2},{4,5},{5,4},{6,7},{7,6},{8,9},{9,8},{10,11... | collective-permute-start | bytes 5701640 | tf_op jit(solution)/shard_map/ppermute | solution.py:23
  80.7 1.8 %collective-permute-done.9 = bf16[928,256]{1,0:T(8,128)(2,1)S(1)} collective-permute-done((bf16[928,256]{1,0:T(8,128)(2,1)}, bf16[928,256]{1,0:T(8,128)(2,1)S(1)}, u32[]{:S(2)}, u32[]{:S(2)}) %collective-permute-start.9) | collective-permute-done | bytes 475168 | tf_op jit(solution)/shard_map/ppermute | solution.py:23
  82.5 10.3 %collective-permute-done.8 = bf16[928,256]{1,0:T(8,128)(2,1)S(1)} collective-permute-done((bf16[928,256]{1,0:T(8,128)(2,1)}, bf16[928,256]{1,0:T(8,128)(2,1)S(1)}, u32[]{:S(2)}, u32[]{:S(2)}) %collective-permute-start.8) | collective-permute-done | bytes 475168 | tf_op jit(solution)/shard_map/ppermute | solution.py:23
  92.7 0.7 collective-permute-done.7
  93.5 0.2 pad_maximum_fusion.1.refs_4_
  93.6 0.0 copy-start.1
  93.6 2.6 %collective-permute-start.10 = (bf16[3,928,256]{2,1,0:T(8,128)(2,1)S(1)}, bf16[3,928,256]{2,1,0:T(8,128)(2,1)}, u32[]{:S(2)}, u32[]{:S(2)}) collective-permute-start(bf16[3,928,256]{2,1,0:T(8,128)(2,1)S(1)} %pad_maximum_fusion.1.refs_4_), channel_id=1, source_target_pairs={{0,1},{1,0},{2,3},{3,2},{4,5},{5,4},{6,7},{7,6},{8,9},{9,8},{10,11... | collective-permute-start | bytes 4276232 | tf_op jit(solution)/shard_map/ppermute | solution.py:23
  96.3 1.9 %collective-permute-start.6 = (bf16[928,256]{1,0:T(8,128)(2,1)}, bf16[928,256]{1,0:T(8,128)(2,1)}, u32[]{:S(2)}, u32[]{:S(2)}) collective-permute-start(bf16[928,256]{1,0:T(8,128)(2,1)} %collective-permute-done.5.refs_2_), channel_id=1, source_target_pairs={{0,1},{1,0},{2,3},{3,2},{4,5},{5,4},{6,7},{7,6},{8,9},{9,8},{10,11... | collective-permute-start | bytes 1425416 | tf_op jit(solution)/shard_map/ppermute | solution.py:23
  98.2 0.6 pad_add_fusion.place_ref
  98.8 1.5 %collective-permute-done.6.refs_3_ = bf16[928,256]{1,0:T(8,128)(2,1)} collective-permute-done((bf16[928,256]{1,0:T(8,128)(2,1)}, bf16[928,256]{1,0:T(8,128)(2,1)}, u32[]{:S(2)}, u32[]{:S(2)}) %collective-permute-start.6) | collective-permute-done | bytes 475168 | tf_op jit(solution)/shard_map/ppermute | solution.py:23
  100.4 0.0 collective-permute-done.10.refs_5_
  100.4 0.0 collective-permute-done.4.refs_1_
  100.4 2.6 %all-gather.2.cloned.1.call-done = bf16[8192,256]{1,0:T(8,128)(2,1)} async-done(((bf16[1024,256]{1,0:T(8,128)(2,1)}), bf16[8192,256]{1,0:T(8,128)(2,1)}) %all-gather.2.cloned.1.call-update) | async-done | bytes 4194320 | tf_op jit(solution)/shard_map/all_gather | solution.py:133
  102.9 0.0 copy-done
  102.9 0.0 copy-done.1
  102.9 8.2 %shard_map.37 = bf16[924,512]{1,0:T(8,128)(2,1)} custom-call(s32[4]{0:T(128)} %pad_add_fusion.place_ref, s32[16]{0:T(128)} %counts_ref.1, bf16[4,928,256]{2,1,0:T(8,128)(2,1)} %copy-done, bf16[4,928,256]{2,1,0:T(8,128)(2,1)} %collective-permute-done.4.refs_1_, bf16[928,256]{1,0:T(8,128)(2,1)} %collective-permute-done.5.refs_2_, ...), custom_call_target="tpu_custom_call" | custom-call | flops 3892314112 | bytes 13631488 | tf_op jit(solution)/shard_map/pallas_call | solution.py:104
Async XLA Ops:
  6.5 96.4 %all-gather.2.cloned.1.call-start = ((), (), s32[]{:S(2)}) async-start(), calls=%async_computation | async-start | bytes 4718592 | tf_op jit(solution)/shard_map/all_gather | solution.py:133
  6.5 9.9 %collective-permute-start = (bf16[256,256]{1,0:T(8,128)(2,1)}, bf16[256,256]{1,0:T(8,128)(2,1)S(1)}, u32[]{:S(2)}, u32[]{:S(2)}) collective-permute-start(bf16[256,256]{1,0:T(8,128)(2,1)} %param.4), channel_id=1, source_target_pairs={{0,0},{1,8},{2,16},{3,24},{4,4},{5,12},{6,20},{7,28},{8,1},{9,9},{... | collective-permute-start | bytes 393224 | tf_op jit(solution)/shard_map/ppermute | solution.py:23
  31.1 25.6 %collective-permute-start.5 = (bf16[928,256]{1,0:T(8,128)(2,1)S(1)}, bf16[928,256]{1,0:T(8,128)(2,1)}, u32[]{:S(2)}, u32[]{:S(2)}) collective-permute-start(bf16[928,256]{1,0:T(8,128)(2,1)S(1)} %pad.4), channel_id=1, source_target_pairs={{0,2},{1,3},{2,0},{3,1},{4,6},{5,7},{6,4},{7,5},{8,10},{9,11},{10,... | collective-permute-start | bytes 1425416 | tf_op jit(solution)/shard_map/ppermute | solution.py:23
  39.7 33.6 %collective-permute-start.3 = (bf16[928,256]{1,0:T(8,128)(2,1)S(1)}, bf16[928,256]{1,0:T(8,128)(2,1)S(1)}, u32[]{:S(2)}, u32[]{:S(2)}) collective-permute-start(bf16[928,256]{1,0:T(8,128)(2,1)S(1)} %pad.4), channel_id=1, source_target_pairs={{0,256},{1,257},{2,258},{3,259},{4,260},{5,261},{6,262},{7,263},{8... | collective-permute-start | bytes 1425416 | tf_op jit(solution)/shard_map/ppermute | solution.py:23
  51.4 24.4 %collective-permute-start.2 = (bf16[928,256]{1,0:T(8,128)(2,1)S(1)}, bf16[928,256]{1,0:T(8,128)(2,1)S(1)}, u32[]{:S(2)}, u32[]{:S(2)}) collective-permute-start(bf16[928,256]{1,0:T(8,128)(2,1)S(1)} %pad.4), channel_id=1, source_target_pairs={{0,384},{1,385},{2,386},{3,387},{4,388},{5,389},{6,390},{7,391},{8... | collective-permute-start | bytes 1425416 | tf_op jit(solution)/shard_map/ppermute | solution.py:23
  53.4 22.4 %collective-permute-start.1 = (bf16[928,256]{1,0:T(8,128)(2,1)S(1)}, bf16[928,256]{1,0:T(8,128)(2,1)S(1)}, u32[]{:S(2)}, u32[]{:S(2)}) collective-permute-start(bf16[928,256]{1,0:T(8,128)(2,1)S(1)} %pad.4), channel_id=1, source_target_pairs={{0,128},{1,129},{2,130},{3,131},{4,132},{5,133},{6,134},{7,135},{8... | collective-permute-start | bytes 1425416 | tf_op jit(solution)/shard_map/ppermute | solution.py:23
  56.7 25.7 %collective-permute-start.9 = (bf16[928,256]{1,0:T(8,128)(2,1)}, bf16[928,256]{1,0:T(8,128)(2,1)S(1)}, u32[]{:S(2)}, u32[]{:S(2)}) collective-permute-start(bf16[928,256]{1,0:T(8,128)(2,1)} %collective-permute-done.5.refs_2_), channel_id=1, source_target_pairs={{0,256},{1,257},{2,258},{3,259},{4,260},{5,261},{6,262},{7,263},{8... | collective-permute-start | bytes 1425416 | tf_op jit(solution)/shard_map/ppermute | solution.py:23
  64.6 28.2 %collective-permute-start.8 = (bf16[928,256]{1,0:T(8,128)(2,1)}, bf16[928,256]{1,0:T(8,128)(2,1)S(1)}, u32[]{:S(2)}, u32[]{:S(2)}) collective-permute-start(bf16[928,256]{1,0:T(8,128)(2,1)} %collective-permute-done.5.refs_2_), channel_id=1, source_target_pairs={{0,384},{1,385},{2,386},{3,387},{4,388},{5,389},{6,390},{7,391},{8... | collective-permute-start | bytes 1425416 | tf_op jit(solution)/shard_map/ppermute | solution.py:23
  73.3 20.1 %collective-permute-start.7 = (bf16[928,256]{1,0:T(8,128)(2,1)}, bf16[928,256]{1,0:T(8,128)(2,1)S(1)}, u32[]{:S(2)}, u32[]{:S(2)}) collective-permute-start(bf16[928,256]{1,0:T(8,128)(2,1)} %collective-permute-done.5.refs_2_), channel_id=1, source_target_pairs={{0,128},{1,129},{2,130},{3,131},{4,132},{5,133},{6,134},{7,135},{8... | collective-permute-start | bytes 1425416 | tf_op jit(solution)/shard_map/ppermute | solution.py:23
  76.1 26.8 %copy-start = (bf16[4,928,256]{2,1,0:T(8,128)(2,1)}, bf16[4,928,256]{2,1,0:T(8,128)(2,1)S(1)}, u32[]{:S(2)}) copy-start(bf16[4,928,256]{2,1,0:T(8,128)(2,1)S(1)} %pad_maximum_fusion.refs_0_) | copy-start | bytes 5701636
  76.1 24.3 %collective-permute-start.4 = (bf16[4,928,256]{2,1,0:T(8,128)(2,1)S(1)}, bf16[4,928,256]{2,1,0:T(8,128)(2,1)}, u32[]{:S(2)}, u32[]{:S(2)}) collective-permute-start(bf16[4,928,256]{2,1,0:T(8,128)(2,1)S(1)} %pad_maximum_fusion.refs_0_), channel_id=1, source_target_pairs={{0,1},{1,0},{2,3},{3,2},{4,5},{5,4},{6,7},{7,6},{8,9},{9,8},{10,11... | collective-permute-start | bytes 5701640 | tf_op jit(solution)/shard_map/ppermute | solution.py:23
  93.6 9.3 %copy-start.1 = (bf16[3,928,256]{2,1,0:T(8,128)(2,1)}, bf16[3,928,256]{2,1,0:T(8,128)(2,1)S(1)}, u32[]{:S(2)}) copy-start(bf16[3,928,256]{2,1,0:T(8,128)(2,1)S(1)} %pad_maximum_fusion.1.refs_4_) | copy-start | bytes 4276228
  93.6 6.7 %collective-permute-start.10 = (bf16[3,928,256]{2,1,0:T(8,128)(2,1)S(1)}, bf16[3,928,256]{2,1,0:T(8,128)(2,1)}, u32[]{:S(2)}, u32[]{:S(2)}) collective-permute-start(bf16[3,928,256]{2,1,0:T(8,128)(2,1)S(1)} %pad_maximum_fusion.1.refs_4_), channel_id=1, source_target_pairs={{0,1},{1,0},{2,3},{3,2},{4,5},{5,4},{6,7},{7,6},{8,9},{9,8},{10,11... | collective-permute-start | bytes 4276232 | tf_op jit(solution)/shard_map/ppermute | solution.py:23
  96.3 4.1 %collective-permute-start.6 = (bf16[928,256]{1,0:T(8,128)(2,1)}, bf16[928,256]{1,0:T(8,128)(2,1)}, u32[]{:S(2)}, u32[]{:S(2)}) collective-permute-start(bf16[928,256]{1,0:T(8,128)(2,1)} %collective-permute-done.5.refs_2_), channel_id=1, source_target_pairs={{0,1},{1,0},{2,3},{3,2},{4,5},{5,4},{6,7},{7,6},{8,9},{9,8},{10,11... | collective-permute-start | bytes 1425416 | tf_op jit(solution)/shard_map/ppermute | solution.py:23
Sparse Core Ops, SparseCore 0:
  31.3 71.6 all-gather.1

commit v4 on v3

--- a/solution.py
+++ b/solution.py
@@ -10,6 +10,7 @@
 ROWBLK = 128
 MROWS = 256
 VMEM = 60 << 20
+AHEAD = 3
 NX, NZ, NYL, NYH, NC = 4, 8, 4, 2, 2
 ALL = ("x", "z", "yl", "yh", "c")
 PLACES = list(itertools.product(range(NX), range(NZ), range(NYL), range(NYH), range(NC)))
@@ -48,48 +49,49 @@
                 arrays.append(array)
     where_is = [[(i, [array is a for a in arrays].index(True)) for i, array in sides] for _, *sides in stashes]
     keys = [key for key, *_ in stashes]
-    pad, ns, ng = arrays[0].shape[-2], len(arrays), len(grads)
+    pad, ns = arrays[0].shape[-2], len(arrays)
 
     def kernel(place_ref, counts_ref, *refs):
-        s_refs, g_refs, (out_ref, s_vm, g_vm, total, s_sem, g_sem) = refs[:ns], refs[ns : ns + ng], refs[ns + ng :]
-        x0, z0, yh0, c0 = (place_ref[i] for i in range(4))
+        s_refs, (g_ref, out_ref, s_vm, g_vm, total, s_sem, g_sem) = refs[:ns], refs[ns:]
+        x0, yh0, c0 = (place_ref[i] for i in range(3))
         own = 2 * x0 + yh0
 
         def q_of(j):
             h, back = keys[j]
             return 2 * lax.rem(x0 - back + NX, NX) + (yh0 if h == 0 else 1 - yh0)
 
-        def grad_copies(j, ref):
+        def core_of(side):
+            return c0 if side == 0 else 1 - c0
+
+        def grad_copies(j):
             return [
                 pltpu.make_async_copy(
-                    ref.at[b],
-                    g_vm.at[j, pl.ds((b // 2) * MROWS, MROWS), pl.ds((b % 2) * MROWS, MROWS)],
+                    g_ref.at[q_of(j) ^ own, 2 * core_of(side) + n],
+                    g_vm.at[j, pl.ds(side * MROWS, MROWS), pl.ds(n * MROWS, MROWS)],
                     g_sem.at[j],
                 )
-                for b in range(NYL)
+                for side in range(NC)
+                for n in range(2)
             ]
 
+        def fetch(j):
+            for copy in grad_copies(j):
+                copy.start()
+            for side, (i, n) in enumerate(where_is[j]):
+                at = s_vm.at[j, :, pl.ds(side * MROWS, MROWS)]
+                pltpu.make_async_copy(s_refs[n] if i is None else s_refs[n].at[i], at, s_sem.at[j]).start()
+
+        for j in range(AHEAD):
+            fetch(j)
         for j in range(len(keys)):
-            if ng == 1:
-                for copy in grad_copies(j, g_refs[0].at[q_of(j) ^ own]):
-                    copy.start()
-            else:
-                for d in range(NZ):
-                    @pl.when((q_of(j) ^ own) == lax.rem(z0 - d * (1 - 2 * c0) + NZ, NZ))
-                    def _():
-                        for copy in grad_copies(j, g_refs[d]):
-                            copy.start()
-            for side, (i, n) in enumerate(where_is[j]):
-                c = c0 if side == 0 else 1 - c0
-                at = s_vm.at[j, :, pl.ds(pl.multiple_of(c * MROWS, MROWS), MROWS)]
-                pltpu.make_async_copy(s_refs[n] if i is None else s_refs[n].at[i], at, s_sem.at[j]).start()
-        for j in range(len(keys)):
-            for copy in grad_copies(j, g_refs[0].at[0] if ng == 1 else g_refs[0]):
+            if j + AHEAD < len(keys):
+                fetch(j + AHEAD)
+            for copy in grad_copies(j):
                 copy.wait()
-            for c in range(NC):
-                @pl.when(counts_ref[2 * q_of(j) + c] < 2)
+            for side in range(NC):
+                @pl.when(counts_ref[2 * q_of(j) + core_of(side)] < 2)
                 def _():
-                    g_vm[j, pl.ds(c * MROWS + ROWBLK, ROWBLK), :] = jnp.zeros((ROWBLK, cols), jnp.bfloat16)
+                    g_vm[j, pl.ds(side * MROWS + ROWBLK, ROWBLK), :] = jnp.zeros((ROWBLK, cols), jnp.bfloat16)
             for c in range(NC):
                 at = s_vm.at[j, :, pl.ds(c * MROWS, MROWS)]
                 pltpu.make_async_copy(at, at, s_sem.at[j]).wait()
@@ -104,7 +106,7 @@
     return pl.pallas_call(
         kernel,
         out_shape=jax.ShapeDtypeStruct((width, cols), jnp.bfloat16),
-        in_specs=[pl.BlockSpec(memory_space=pltpu.SMEM)] * 2 + [pl.BlockSpec(memory_space=pl.ANY)] * (ns + ng),
+        in_specs=[pl.BlockSpec(memory_space=pltpu.SMEM)] * 2 + [pl.BlockSpec(memory_space=pl.ANY)] * (ns + 1),
         out_specs=pl.BlockSpec(memory_space=pltpu.VMEM),
         scratch_shapes=[
             pltpu.VMEM((NZ, pad, rows), jnp.bfloat16),
@@ -115,7 +117,7 @@
         ],
         compiler_params=pltpu.CompilerParams(vmem_limit_bytes=VMEM),
         cost_estimate=pl.CostEstimate(flops=16 * pad * rows * cols, bytes_accessed=13 << 20, transcendentals=0),
-    )(place, counts, *arrays, *grads)
+    )(place, counts, *arrays, grads)
 
 
 def together(*values):
@@ -123,14 +125,14 @@
 
 
 def shards(stash, out_grads, block_counts):
-    place = jnp.stack([lax.axis_index(a) for a in ("x", "z", "yh", "c")]).astype(jnp.int32)
+    place = jnp.stack([lax.axis_index(a) for a in ("x", "yh", "c")]).astype(jnp.int32)
     width = stash.shape[1]
     own = jnp.pad(stash.T, ((0, -width % 32), (0, 0)))
 
     near = permute(out_grads, to_owner_plane)
     near, own = together(near, own)
     piece = lax.all_gather(near, "yl", axis=0, tiled=True)
-    grads = [lax.all_gather(piece, "z", axis=0, tiled=True).reshape(NZ, NYL, MROWS, MROWS)]
+    grads = lax.all_gather(piece, "z", axis=0, tiled=True).reshape(NZ, NYL, MROWS, MROWS)
 
     piece, own = together(piece, own)
     partner = permute(own, other_half)

time: 118 us -> 118 us (level)
  no operation moved by 1% of the time
where the time goes in v4:
time: 118 us
  starting transfers between devices  59.4 us (50%)
  waiting for transfers between devices  20 us (17%)
  blocking collectives  14.7 us (12%)
  between operations  13.6 us (12%)
  Pallas kernels  7.91 us (7%)
    ppermute x11, starting transfers between devices, permute(): lax.ppermute(value, ALL, [(linear(*p), linear(*target(*p))) for p in PLAC...  59.4 us
    ppermute x11, waiting for transfers between devices, permute(): lax.ppermute(value, ALL, [(linear(*p), linear(*target(*p))) for p in PLAC...  17.5 us
    all_gather x1, blocking collectives, shards(): piece = lax.all_gather(near, 'yl', axis=0, tiled=True)  14.7 us
    pallas_call x1, Pallas kernels, product(): pl.pallas_call(kernel, out_shape=jax.ShapeDtypeStruct((width, cols), jnp....  7.91 us
    all_gather x1, waiting for transfers between devices, shards(): lax.all_gather(piece, 'z', axis=0, tiled=True)  2.56 us
  transfers between devices with their start and end apart: 12, of which 6 were waited for; matrix products, arithmetic and copies ran while one was open for 2% of the time, Pallas kernels for 0%

profile of v4, /device:TPU:1, one launch (start us, length us, event | category | flops | bytes accessed | tf_op | source)
XLA Modules:
  0.0 117.7 jit_solution(12123912321474632470)
XLA Ops:
  6.5 0.0 all-gather.2.cloned.1.call-start
  6.5 5.6 %collective-permute-start = (bf16[256,256]{1,0:T(8,128)(2,1)}, bf16[256,256]{1,0:T(8,128)(2,1)S(1)}, u32[]{:S(2)}, u32[]{:S(2)}) collective-permute-start(bf16[256,256]{1,0:T(8,128)(2,1)} %param.4), channel_id=1, source_target_pairs={{0,0},{1,8},{2,16},{3,24},{4,4},{5,12},{6,20},{7,28},{8,1},{9,9},{... | collective-permute-start | bytes 393224 | tf_op jit(solution)/shard_map/ppermute | solution.py:24
  12.1 1.1 pad.4
  13.2 3.2 %collective-permute-done = bf16[256,256]{1,0:T(8,128)(2,1)S(1)} collective-permute-done((bf16[256,256]{1,0:T(8,128)(2,1)}, bf16[256,256]{1,0:T(8,128)(2,1)S(1)}, u32[]{:S(2)}, u32[]{:S(2)}) %collective-permute-start) | collective-permute-done | bytes 131104 | tf_op jit(solution)/shard_map/ppermute | solution.py:24
  16.4 14.7 %all_gather.6 = bf16[1024,256]{1,0:T(8,128)(2,1)} all-gather(bf16[256,256]{1,0:T(8,128)(2,1)S(1)} %collective-permute-done), channel_id=1, replica_groups=mesh['x'=4,'z'=8,'yl'=4,'yh'=2,'c'=2] {'yl'}, dimensions={0}, use_global_device_ids=true | all-gather | bytes 655360 | tf_op jit(solution)/shard_map/all_gather | solution.py:134
  31.1 0.0 all-gather.2.cloned.1.call-update
  31.1 8.6 %collective-permute-start.5 = (bf16[928,256]{1,0:T(8,128)(2,1)S(1)}, bf16[928,256]{1,0:T(8,128)(2,1)}, u32[]{:S(2)}, u32[]{:S(2)}) collective-permute-start(bf16[928,256]{1,0:T(8,128)(2,1)S(1)} %pad.4), channel_id=1, source_target_pairs={{0,2},{1,3},{2,0},{3,1},{4,6},{5,7},{6,4},{7,5},{8,10},{9,11},{10,... | collective-permute-start | bytes 1425416 | tf_op jit(solution)/shard_map/ppermute | solution.py:24
  39.7 11.7 %collective-permute-start.3 = (bf16[928,256]{1,0:T(8,128)(2,1)S(1)}, bf16[928,256]{1,0:T(8,128)(2,1)S(1)}, u32[]{:S(2)}, u32[]{:S(2)}) collective-permute-start(bf16[928,256]{1,0:T(8,128)(2,1)S(1)} %pad.4), channel_id=1, source_target_pairs={{0,256},{1,257},{2,258},{3,259},{4,260},{5,261},{6,262},{7,263},{8... | collective-permute-start | bytes 1425416 | tf_op jit(solution)/shard_map/ppermute | solution.py:24
  51.4 1.9 %collective-permute-start.2 = (bf16[928,256]{1,0:T(8,128)(2,1)S(1)}, bf16[928,256]{1,0:T(8,128)(2,1)S(1)}, u32[]{:S(2)}, u32[]{:S(2)}) collective-permute-start(bf16[928,256]{1,0:T(8,128)(2,1)S(1)} %pad.4), channel_id=1, source_target_pairs={{0,384},{1,385},{2,386},{3,387},{4,388},{5,389},{6,390},{7,391},{8... | collective-permute-start | bytes 1425416 | tf_op jit(solution)/shard_map/ppermute | solution.py:24
  53.4 3.4 %collective-permute-start.1 = (bf16[928,256]{1,0:T(8,128)(2,1)S(1)}, bf16[928,256]{1,0:T(8,128)(2,1)S(1)}, u32[]{:S(2)}, u32[]{:S(2)}) collective-permute-start(bf16[928,256]{1,0:T(8,128)(2,1)S(1)} %pad.4), channel_id=1, source_target_pairs={{0,128},{1,129},{2,130},{3,131},{4,132},{5,133},{6,134},{7,135},{8... | collective-permute-start | bytes 1425416 | tf_op jit(solution)/shard_map/ppermute | solution.py:24
  56.7 0.0 collective-permute-done.5.refs_2_
  56.7 7.8 %collective-permute-start.9 = (bf16[928,256]{1,0:T(8,128)(2,1)}, bf16[928,256]{1,0:T(8,128)(2,1)S(1)}, u32[]{:S(2)}, u32[]{:S(2)}) collective-permute-start(bf16[928,256]{1,0:T(8,128)(2,1)} %collective-permute-done.5.refs_2_), channel_id=1, source_target_pairs={{0,256},{1,257},{2,258},{3,259},{4,260},{5,261},{6,262},{7,263},{8... | collective-permute-start | bytes 1425416 | tf_op jit(solution)/shard_map/ppermute | solution.py:24
  64.6 8.7 %collective-permute-start.8 = (bf16[928,256]{1,0:T(8,128)(2,1)}, bf16[928,256]{1,0:T(8,128)(2,1)S(1)}, u32[]{:S(2)}, u32[]{:S(2)}) collective-permute-start(bf16[928,256]{1,0:T(8,128)(2,1)} %collective-permute-done.5.refs_2_), channel_id=1, source_target_pairs={{0,384},{1,385},{2,386},{3,387},{4,388},{5,389},{6,390},{7,391},{8... | collective-permute-start | bytes 1425416 | tf_op jit(solution)/shard_map/ppermute | solution.py:24
  73.3 0.0 collective-permute-done.3
  73.3 2.5 %collective-permute-start.7 = (bf16[928,256]{1,0:T(8,128)(2,1)}, bf16[928,256]{1,0:T(8,128)(2,1)S(1)}, u32[]{:S(2)}, u32[]{:S(2)}) collective-permute-start(bf16[928,256]{1,0:T(8,128)(2,1)} %collective-permute-done.5.refs_2_), channel_id=1, source_target_pairs={{0,128},{1,129},{2,130},{3,131},{4,132},{5,133},{6,134},{7,135},{8... | collective-permute-start | bytes 1425416 | tf_op jit(solution)/shard_map/ppermute | solution.py:24
  75.8 0.0 collective-permute-done.2
  75.8 0.0 collective-permute-done.1
  75.8 0.2 pad_maximum_fusion.refs_0_
  76.1 0.0 copy-start
  76.1 4.6 %collective-permute-start.4 = (bf16[4,928,256]{2,1,0:T(8,128)(2,1)S(1)}, bf16[4,928,256]{2,1,0:T(8,128)(2,1)}, u32[]{:S(2)}, u32[]{:S(2)}) collective-permute-start(bf16[4,928,256]{2,1,0:T(8,128)(2,1)S(1)} %pad_maximum_fusion.refs_0_), channel_id=1, source_target_pairs={{0,1},{1,0},{2,3},{3,2},{4,5},{5,4},{6,7},{7,6},{8,9},{9,8},{10,11... | collective-permute-start | bytes 5701640 | tf_op jit(solution)/shard_map/ppermute | solution.py:24
  80.7 1.8 %collective-permute-done.9 = bf16[928,256]{1,0:T(8,128)(2,1)S(1)} collective-permute-done((bf16[928,256]{1,0:T(8,128)(2,1)}, bf16[928,256]{1,0:T(8,128)(2,1)S(1)}, u32[]{:S(2)}, u32[]{:S(2)}) %collective-permute-start.9) | collective-permute-done | bytes 475168 | tf_op jit(solution)/shard_map/ppermute | solution.py:24
  82.5 10.3 %collective-permute-done.8 = bf16[928,256]{1,0:T(8,128)(2,1)S(1)} collective-permute-done((bf16[928,256]{1,0:T(8,128)(2,1)}, bf16[928,256]{1,0:T(8,128)(2,1)S(1)}, u32[]{:S(2)}, u32[]{:S(2)}) %collective-permute-start.8) | collective-permute-done | bytes 475168 | tf_op jit(solution)/shard_map/ppermute | solution.py:24
  92.7 0.7 collective-permute-done.7
  93.5 0.2 pad_maximum_fusion.1.refs_4_
  93.6 0.0 copy-start.1
  93.6 2.6 %collective-permute-start.10 = (bf16[3,928,256]{2,1,0:T(8,128)(2,1)S(1)}, bf16[3,928,256]{2,1,0:T(8,128)(2,1)}, u32[]{:S(2)}, u32[]{:S(2)}) collective-permute-start(bf16[3,928,256]{2,1,0:T(8,128)(2,1)S(1)} %pad_maximum_fusion.1.refs_4_), channel_id=1, source_target_pairs={{0,1},{1,0},{2,3},{3,2},{4,5},{5,4},{6,7},{7,6},{8,9},{9,8},{10,11... | collective-permute-start | bytes 4276232 | tf_op jit(solution)/shard_map/ppermute | solution.py:24
  96.3 1.9 %collective-permute-start.6 = (bf16[928,256]{1,0:T(8,128)(2,1)}, bf16[928,256]{1,0:T(8,128)(2,1)}, u32[]{:S(2)}, u32[]{:S(2)}) collective-permute-start(bf16[928,256]{1,0:T(8,128)(2,1)} %collective-permute-done.5.refs_2_), channel_id=1, source_target_pairs={{0,1},{1,0},{2,3},{3,2},{4,5},{5,4},{6,7},{7,6},{8,9},{9,8},{10,11... | collective-permute-start | bytes 1425416 | tf_op jit(solution)/shard_map/ppermute | solution.py:24
  98.2 0.6 pad_add_fusion.place_ref
  98.8 1.5 %collective-permute-done.6.refs_3_ = bf16[928,256]{1,0:T(8,128)(2,1)} collective-permute-done((bf16[928,256]{1,0:T(8,128)(2,1)}, bf16[928,256]{1,0:T(8,128)(2,1)}, u32[]{:S(2)}, u32[]{:S(2)}) %collective-permute-start.6) | collective-permute-done | bytes 475168 | tf_op jit(solution)/shard_map/ppermute | solution.py:24
  100.4 0.0 collective-permute-done.10.refs_5_
  100.4 0.0 collective-permute-done.4.refs_1_
  100.4 2.6 %all-gather.2.cloned.1.call-done = bf16[8192,256]{1,0:T(8,128)(2,1)} async-done(((bf16[1024,256]{1,0:T(8,128)(2,1)}), bf16[8192,256]{1,0:T(8,128)(2,1)}) %all-gather.2.cloned.1.call-update) | async-done | bytes 4194320 | tf_op jit(solution)/shard_map/all_gather | solution.py:135
  102.9 0.0 copy-done
  102.9 0.0 copy-done.1
  102.9 7.9 %shard_map.37 = bf16[924,512]{1,0:T(8,128)(2,1)} custom-call(s32[3]{0:T(128)} %pad_add_fusion.place_ref, s32[16]{0:T(128)} %counts_ref.1, bf16[4,928,256]{2,1,0:T(8,128)(2,1)} %copy-done, bf16[4,928,256]{2,1,0:T(8,128)(2,1)} %collective-permute-done.4.refs_1_, bf16[928,256]{1,0:T(8,128)(2,1)} %collective-permute-done.5.refs_2_, ...), custom_call_target="tpu_custom_call" | custom-call | flops 3892314112 | bytes 13631488 | tf_op jit(solution)/shard_map/pallas_call | solution.py:106
Async XLA Ops:
  6.5 96.4 %all-gather.2.cloned.1.call-start = ((), (), s32[]{:S(2)}) async-start(), calls=%async_computation | async-start | bytes 4718592 | tf_op jit(solution)/shard_map/all_gather | solution.py:135
  6.5 9.9 %collective-permute-start = (bf16[256,256]{1,0:T(8,128)(2,1)}, bf16[256,256]{1,0:T(8,128)(2,1)S(1)}, u32[]{:S(2)}, u32[]{:S(2)}) collective-permute-start(bf16[256,256]{1,0:T(8,128)(2,1)} %param.4), channel_id=1, source_target_pairs={{0,0},{1,8},{2,16},{3,24},{4,4},{5,12},{6,20},{7,28},{8,1},{9,9},{... | collective-permute-start | bytes 393224 | tf_op jit(solution)/shard_map/ppermute | solution.py:24
  31.1 25.6 %collective-permute-start.5 = (bf16[928,256]{1,0:T(8,128)(2,1)S(1)}, bf16[928,256]{1,0:T(8,128)(2,1)}, u32[]{:S(2)}, u32[]{:S(2)}) collective-permute-start(bf16[928,256]{1,0:T(8,128)(2,1)S(1)} %pad.4), channel_id=1, source_target_pairs={{0,2},{1,3},{2,0},{3,1},{4,6},{5,7},{6,4},{7,5},{8,10},{9,11},{10,... | collective-permute-start | bytes 1425416 | tf_op jit(solution)/shard_map/ppermute | solution.py:24
  39.7 33.6 %collective-permute-start.3 = (bf16[928,256]{1,0:T(8,128)(2,1)S(1)}, bf16[928,256]{1,0:T(8,128)(2,1)S(1)}, u32[]{:S(2)}, u32[]{:S(2)}) collective-permute-start(bf16[928,256]{1,0:T(8,128)(2,1)S(1)} %pad.4), channel_id=1, source_target_pairs={{0,256},{1,257},{2,258},{3,259},{4,260},{5,261},{6,262},{7,263},{8... | collective-permute-start | bytes 1425416 | tf_op jit(solution)/shard_map/ppermute | solution.py:24
  51.4 24.4 %collective-permute-start.2 = (bf16[928,256]{1,0:T(8,128)(2,1)S(1)}, bf16[928,256]{1,0:T(8,128)(2,1)S(1)}, u32[]{:S(2)}, u32[]{:S(2)}) collective-permute-start(bf16[928,256]{1,0:T(8,128)(2,1)S(1)} %pad.4), channel_id=1, source_target_pairs={{0,384},{1,385},{2,386},{3,387},{4,388},{5,389},{6,390},{7,391},{8... | collective-permute-start | bytes 1425416 | tf_op jit(solution)/shard_map/ppermute | solution.py:24
  53.4 22.4 %collective-permute-start.1 = (bf16[928,256]{1,0:T(8,128)(2,1)S(1)}, bf16[928,256]{1,0:T(8,128)(2,1)S(1)}, u32[]{:S(2)}, u32[]{:S(2)}) collective-permute-start(bf16[928,256]{1,0:T(8,128)(2,1)S(1)} %pad.4), channel_id=1, source_target_pairs={{0,128},{1,129},{2,130},{3,131},{4,132},{5,133},{6,134},{7,135},{8... | collective-permute-start | bytes 1425416 | tf_op jit(solution)/shard_map/ppermute | solution.py:24
  56.7 25.7 %collective-permute-start.9 = (bf16[928,256]{1,0:T(8,128)(2,1)}, bf16[928,256]{1,0:T(8,128)(2,1)S(1)}, u32[]{:S(2)}, u32[]{:S(2)}) collective-permute-start(bf16[928,256]{1,0:T(8,128)(2,1)} %collective-permute-done.5.refs_2_), channel_id=1, source_target_pairs={{0,256},{1,257},{2,258},{3,259},{4,260},{5,261},{6,262},{7,263},{8... | collective-permute-start | bytes 1425416 | tf_op jit(solution)/shard_map/ppermute | solution.py:24
  64.6 28.2 %collective-permute-start.8 = (bf16[928,256]{1,0:T(8,128)(2,1)}, bf16[928,256]{1,0:T(8,128)(2,1)S(1)}, u32[]{:S(2)}, u32[]{:S(2)}) collective-permute-start(bf16[928,256]{1,0:T(8,128)(2,1)} %collective-permute-done.5.refs_2_), channel_id=1, source_target_pairs={{0,384},{1,385},{2,386},{3,387},{4,388},{5,389},{6,390},{7,391},{8... | collective-permute-start | bytes 1425416 | tf_op jit(solution)/shard_map/ppermute | solution.py:24
  73.3 20.1 %collective-permute-start.7 = (bf16[928,256]{1,0:T(8,128)(2,1)}, bf16[928,256]{1,0:T(8,128)(2,1)S(1)}, u32[]{:S(2)}, u32[]{:S(2)}) collective-permute-start(bf16[928,256]{1,0:T(8,128)(2,1)} %collective-permute-done.5.refs_2_), channel_id=1, source_target_pairs={{0,128},{1,129},{2,130},{3,131},{4,132},{5,133},{6,134},{7,135},{8... | collective-permute-start | bytes 1425416 | tf_op jit(solution)/shard_map/ppermute | solution.py:24
  76.1 26.8 %copy-start = (bf16[4,928,256]{2,1,0:T(8,128)(2,1)}, bf16[4,928,256]{2,1,0:T(8,128)(2,1)S(1)}, u32[]{:S(2)}) copy-start(bf16[4,928,256]{2,1,0:T(8,128)(2,1)S(1)} %pad_maximum_fusion.refs_0_) | copy-start | bytes 5701636
  76.1 24.3 %collective-permute-start.4 = (bf16[4,928,256]{2,1,0:T(8,128)(2,1)S(1)}, bf16[4,928,256]{2,1,0:T(8,128)(2,1)}, u32[]{:S(2)}, u32[]{:S(2)}) collective-permute-start(bf16[4,928,256]{2,1,0:T(8,128)(2,1)S(1)} %pad_maximum_fusion.refs_0_), channel_id=1, source_target_pairs={{0,1},{1,0},{2,3},{3,2},{4,5},{5,4},{6,7},{7,6},{8,9},{9,8},{10,11... | collective-permute-start | bytes 5701640 | tf_op jit(solution)/shard_map/ppermute | solution.py:24
  93.6 9.3 %copy-start.1 = (bf16[3,928,256]{2,1,0:T(8,128)(2,1)}, bf16[3,928,256]{2,1,0:T(8,128)(2,1)S(1)}, u32[]{:S(2)}) copy-start(bf16[3,928,256]{2,1,0:T(8,128)(2,1)S(1)} %pad_maximum_fusion.1.refs_4_) | copy-start | bytes 4276228
  93.6 6.7 %collective-permute-start.10 = (bf16[3,928,256]{2,1,0:T(8,128)(2,1)S(1)}, bf16[3,928,256]{2,1,0:T(8,128)(2,1)}, u32[]{:S(2)}, u32[]{:S(2)}) collective-permute-start(bf16[3,928,256]{2,1,0:T(8,128)(2,1)S(1)} %pad_maximum_fusion.1.refs_4_), channel_id=1, source_target_pairs={{0,1},{1,0},{2,3},{3,2},{4,5},{5,4},{6,7},{7,6},{8,9},{9,8},{10,11... | collective-permute-start | bytes 4276232 | tf_op jit(solution)/shard_map/ppermute | solution.py:24
  96.3 4.1 %collective-permute-start.6 = (bf16[928,256]{1,0:T(8,128)(2,1)}, bf16[928,256]{1,0:T(8,128)(2,1)}, u32[]{:S(2)}, u32[]{:S(2)}) collective-permute-start(bf16[928,256]{1,0:T(8,128)(2,1)} %collective-permute-done.5.refs_2_), channel_id=1, source_target_pairs={{0,1},{1,0},{2,3},{3,2},{4,5},{5,4},{6,7},{7,6},{8,9},{9,8},{10,11... | collective-permute-start | bytes 1425416 | tf_op jit(solution)/shard_map/ppermute | solution.py:24
Sparse Core Ops, SparseCore 0:
  31.3 71.6 all-gather.1

commit v5 on v4

--- a/solution.py
+++ b/solution.py
@@ -63,38 +63,50 @@
         def core_of(side):
             return c0 if side == 0 else 1 - c0
 
-        def grad_copies(j):
-            return [
+        def core_of(side):
+            return c0 if side == 0 else 1 - c0
+
+        def live(j, side):
+            return counts_ref[2 * q_of(j) + core_of(side)] >= 2
+
+        def copies(j, side, size):
+            i, n = where_is[j][side]
+            found = [
                 pltpu.make_async_copy(
-                    g_ref.at[q_of(j) ^ own, 2 * core_of(side) + n],
-                    g_vm.at[j, pl.ds(side * MROWS, MROWS), pl.ds(n * MROWS, MROWS)],
+                    g_ref.at[q_of(j) ^ own, 2 * core_of(side) + h, pl.ds(0, size), :],
+                    g_vm.at[j, pl.ds(side * MROWS, size), pl.ds(h * MROWS, MROWS)],
                     g_sem.at[j],
                 )
-                for side in range(NC)
-                for n in range(2)
+                for h in range(2)
             ]
+            source = s_refs[n] if i is None else s_refs[n].at[i]
+            at = s_vm.at[j, :, pl.ds(side * MROWS, size)]
+            return [*found, pltpu.make_async_copy(source.at[:, pl.ds(0, size)], at, s_sem.at[j])]
+
+        def each(j, side, act):
+            for size, chosen in ((MROWS, live(j, side)), (ROWBLK, jnp.logical_not(live(j, side)))):
+                @pl.when(chosen)
+                def _():
+                    for copy in copies(j, side, size):
+                        act(copy)
 
         def fetch(j):
-            for copy in grad_copies(j):
-                copy.start()
-            for side, (i, n) in enumerate(where_is[j]):
-                at = s_vm.at[j, :, pl.ds(side * MROWS, MROWS)]
-                pltpu.make_async_copy(s_refs[n] if i is None else s_refs[n].at[i], at, s_sem.at[j]).start()
+            for side in range(NC):
+                each(j, side, lambda copy: copy.start())
+
+                @pl.when(jnp.logical_not(live(j, side)))
+                def _():
+                    dead = pl.ds(side * MROWS + ROWBLK, ROWBLK)
+                    g_vm[j, dead, :] = jnp.zeros((ROWBLK, cols), jnp.bfloat16)
+                    s_vm[j, :, dead] = jnp.zeros((pad, ROWBLK), jnp.bfloat16)
 
         for j in range(AHEAD):
             fetch(j)
         for j in range(len(keys)):
             if j + AHEAD < len(keys):
                 fetch(j + AHEAD)
-            for copy in grad_copies(j):
-                copy.wait()
             for side in range(NC):
-                @pl.when(counts_ref[2 * q_of(j) + core_of(side)] < 2)
-                def _():
-                    g_vm[j, pl.ds(side * MROWS + ROWBLK, ROWBLK), :] = jnp.zeros((ROWBLK, cols), jnp.bfloat16)
-            for c in range(NC):
-                at = s_vm.at[j, :, pl.ds(c * MROWS, MROWS)]
-                pltpu.make_async_copy(at, at, s_sem.at[j]).wait()
+                each(j, side, lambda copy: copy.wait())
             part = jnp.dot(s_vm[j], g_vm[j], preferred_element_type=jnp.float32)
             if j == 0:
                 total[...] = part

time: 118 us -> 118 us (level)
  no operation moved by 1% of the time
where the time goes in v5:
time: 118 us
  starting transfers between devices  59.4 us (50%)
  waiting for transfers between devices  20 us (17%)
  blocking collectives  14.7 us (12%)
  between operations  13.6 us (12%)
  Pallas kernels  7.76 us (7%)
    ppermute x11, starting transfers between devices, permute(): lax.ppermute(value, ALL, [(linear(*p), linear(*target(*p))) for p in PLAC...  59.4 us
    ppermute x11, waiting for transfers between devices, permute(): lax.ppermute(value, ALL, [(linear(*p), linear(*target(*p))) for p in PLAC...  17.5 us
    all_gather x1, blocking collectives, shards(): piece = lax.all_gather(near, 'yl', axis=0, tiled=True)  14.7 us
    pallas_call x1, Pallas kernels, product(): pl.pallas_call(kernel, out_shape=jax.ShapeDtypeStruct((width, cols), jnp....  7.76 us
    all_gather x1, waiting for transfers between devices, shards(): lax.all_gather(piece, 'z', axis=0, tiled=True)  2.56 us
  transfers between devices with their start and end apart: 12, of which 6 were waited for; matrix products, arithmetic and copies ran while one was open for 2% of the time, Pallas kernels for 0%

profile of v5, /device:TPU:1, one launch (start us, length us, event | category | flops | bytes accessed | tf_op | source)
XLA Modules:
  0.0 117.5 jit_solution(3114440713533109625)
XLA Ops:
  6.5 0.0 all-gather.2.cloned.1.call-start
  6.5 5.6 %collective-permute-start = (bf16[256,256]{1,0:T(8,128)(2,1)}, bf16[256,256]{1,0:T(8,128)(2,1)S(1)}, u32[]{:S(2)}, u32[]{:S(2)}) collective-permute-start(bf16[256,256]{1,0:T(8,128)(2,1)} %param.4), channel_id=1, source_target_pairs={{0,0},{1,8},{2,16},{3,24},{4,4},{5,12},{6,20},{7,28},{8,1},{9,9},{... | collective-permute-start | bytes 393224 | tf_op jit(solution)/shard_map/ppermute | solution.py:24
  12.1 1.1 pad.4
  13.2 3.2 %collective-permute-done = bf16[256,256]{1,0:T(8,128)(2,1)S(1)} collective-permute-done((bf16[256,256]{1,0:T(8,128)(2,1)}, bf16[256,256]{1,0:T(8,128)(2,1)S(1)}, u32[]{:S(2)}, u32[]{:S(2)}) %collective-permute-start) | collective-permute-done | bytes 131104 | tf_op jit(solution)/shard_map/ppermute | solution.py:24
  16.4 14.7 %all_gather.6 = bf16[1024,256]{1,0:T(8,128)(2,1)} all-gather(bf16[256,256]{1,0:T(8,128)(2,1)S(1)} %collective-permute-done), channel_id=1, replica_groups=mesh['x'=4,'z'=8,'yl'=4,'yh'=2,'c'=2] {'yl'}, dimensions={0}, use_global_device_ids=true | all-gather | bytes 655360 | tf_op jit(solution)/shard_map/all_gather | solution.py:146
  31.1 0.0 all-gather.2.cloned.1.call-update
  31.1 8.6 %collective-permute-start.5 = (bf16[928,256]{1,0:T(8,128)(2,1)S(1)}, bf16[928,256]{1,0:T(8,128)(2,1)}, u32[]{:S(2)}, u32[]{:S(2)}) collective-permute-start(bf16[928,256]{1,0:T(8,128)(2,1)S(1)} %pad.4), channel_id=1, source_target_pairs={{0,2},{1,3},{2,0},{3,1},{4,6},{5,7},{6,4},{7,5},{8,10},{9,11},{10,... | collective-permute-start | bytes 1425416 | tf_op jit(solution)/shard_map/ppermute | solution.py:24
  39.7 11.7 %collective-permute-start.3 = (bf16[928,256]{1,0:T(8,128)(2,1)S(1)}, bf16[928,256]{1,0:T(8,128)(2,1)S(1)}, u32[]{:S(2)}, u32[]{:S(2)}) collective-permute-start(bf16[928,256]{1,0:T(8,128)(2,1)S(1)} %pad.4), channel_id=1, source_target_pairs={{0,256},{1,257},{2,258},{3,259},{4,260},{5,261},{6,262},{7,263},{8... | collective-permute-start | bytes 1425416 | tf_op jit(solution)/shard_map/ppermute | solution.py:24
  51.4 1.9 %collective-permute-start.2 = (bf16[928,256]{1,0:T(8,128)(2,1)S(1)}, bf16[928,256]{1,0:T(8,128)(2,1)S(1)}, u32[]{:S(2)}, u32[]{:S(2)}) collective-permute-start(bf16[928,256]{1,0:T(8,128)(2,1)S(1)} %pad.4), channel_id=1, source_target_pairs={{0,384},{1,385},{2,386},{3,387},{4,388},{5,389},{6,390},{7,391},{8... | collective-permute-start | bytes 1425416 | tf_op jit(solution)/shard_map/ppermute | solution.py:24
  53.4 3.4 %collective-permute-start.1 = (bf16[928,256]{1,0:T(8,128)(2,1)S(1)}, bf16[928,256]{1,0:T(8,128)(2,1)S(1)}, u32[]{:S(2)}, u32[]{:S(2)}) collective-permute-start(bf16[928,256]{1,0:T(8,128)(2,1)S(1)} %pad.4), channel_id=1, source_target_pairs={{0,128},{1,129},{2,130},{3,131},{4,132},{5,133},{6,134},{7,135},{8... | collective-permute-start | bytes 1425416 | tf_op jit(solution)/shard_map/ppermute | solution.py:24
  56.7 0.0 collective-permute-done.5.refs_2_
  56.7 7.8 %collective-permute-start.9 = (bf16[928,256]{1,0:T(8,128)(2,1)}, bf16[928,256]{1,0:T(8,128)(2,1)S(1)}, u32[]{:S(2)}, u32[]{:S(2)}) collective-permute-start(bf16[928,256]{1,0:T(8,128)(2,1)} %collective-permute-done.5.refs_2_), channel_id=1, source_target_pairs={{0,256},{1,257},{2,258},{3,259},{4,260},{5,261},{6,262},{7,263},{8... | collective-permute-start | bytes 1425416 | tf_op jit(solution)/shard_map/ppermute | solution.py:24
  64.6 8.7 %collective-permute-start.8 = (bf16[928,256]{1,0:T(8,128)(2,1)}, bf16[928,256]{1,0:T(8,128)(2,1)S(1)}, u32[]{:S(2)}, u32[]{:S(2)}) collective-permute-start(bf16[928,256]{1,0:T(8,128)(2,1)} %collective-permute-done.5.refs_2_), channel_id=1, source_target_pairs={{0,384},{1,385},{2,386},{3,387},{4,388},{5,389},{6,390},{7,391},{8... | collective-permute-start | bytes 1425416 | tf_op jit(solution)/shard_map/ppermute | solution.py:24
  73.3 0.0 collective-permute-done.3
  73.3 2.5 %collective-permute-start.7 = (bf16[928,256]{1,0:T(8,128)(2,1)}, bf16[928,256]{1,0:T(8,128)(2,1)S(1)}, u32[]{:S(2)}, u32[]{:S(2)}) collective-permute-start(bf16[928,256]{1,0:T(8,128)(2,1)} %collective-permute-done.5.refs_2_), channel_id=1, source_target_pairs={{0,128},{1,129},{2,130},{3,131},{4,132},{5,133},{6,134},{7,135},{8... | collective-permute-start | bytes 1425416 | tf_op jit(solution)/shard_map/ppermute | solution.py:24
  75.8 0.0 collective-permute-done.2
  75.8 0.0 collective-permute-done.1
  75.8 0.2 pad_maximum_fusion.refs_0_
  76.1 0.0 copy-start
  76.1 4.6 %collective-permute-start.4 = (bf16[4,928,256]{2,1,0:T(8,128)(2,1)S(1)}, bf16[4,928,256]{2,1,0:T(8,128)(2,1)}, u32[]{:S(2)}, u32[]{:S(2)}) collective-permute-start(bf16[4,928,256]{2,1,0:T(8,128)(2,1)S(1)} %pad_maximum_fusion.refs_0_), channel_id=1, source_target_pairs={{0,1},{1,0},{2,3},{3,2},{4,5},{5,4},{6,7},{7,6},{8,9},{9,8},{10,11... | collective-permute-start | bytes 5701640 | tf_op jit(solution)/shard_map/ppermute | solution.py:24
  80.7 1.8 %collective-permute-done.9 = bf16[928,256]{1,0:T(8,128)(2,1)S(1)} collective-permute-done((bf16[928,256]{1,0:T(8,128)(2,1)}, bf16[928,256]{1,0:T(8,128)(2,1)S(1)}, u32[]{:S(2)}, u32[]{:S(2)}) %collective-permute-start.9) | collective-permute-done | bytes 475168 | tf_op jit(solution)/shard_map/ppermute | solution.py:24
  82.5 10.3 %collective-permute-done.8 = bf16[928,256]{1,0:T(8,128)(2,1)S(1)} collective-permute-done((bf16[928,256]{1,0:T(8,128)(2,1)}, bf16[928,256]{1,0:T(8,128)(2,1)S(1)}, u32[]{:S(2)}, u32[]{:S(2)}) %collective-permute-start.8) | collective-permute-done | bytes 475168 | tf_op jit(solution)/shard_map/ppermute | solution.py:24
  92.7 0.7 collective-permute-done.7
  93.5 0.2 pad_maximum_fusion.1.refs_4_
  93.6 0.0 copy-start.1
  93.6 2.6 %collective-permute-start.10 = (bf16[3,928,256]{2,1,0:T(8,128)(2,1)S(1)}, bf16[3,928,256]{2,1,0:T(8,128)(2,1)}, u32[]{:S(2)}, u32[]{:S(2)}) collective-permute-start(bf16[3,928,256]{2,1,0:T(8,128)(2,1)S(1)} %pad_maximum_fusion.1.refs_4_), channel_id=1, source_target_pairs={{0,1},{1,0},{2,3},{3,2},{4,5},{5,4},{6,7},{7,6},{8,9},{9,8},{10,11... | collective-permute-start | bytes 4276232 | tf_op jit(solution)/shard_map/ppermute | solution.py:24
  96.3 1.9 %collective-permute-start.6 = (bf16[928,256]{1,0:T(8,128)(2,1)}, bf16[928,256]{1,0:T(8,128)(2,1)}, u32[]{:S(2)}, u32[]{:S(2)}) collective-permute-start(bf16[928,256]{1,0:T(8,128)(2,1)} %collective-permute-done.5.refs_2_), channel_id=1, source_target_pairs={{0,1},{1,0},{2,3},{3,2},{4,5},{5,4},{6,7},{7,6},{8,9},{9,8},{10,11... | collective-permute-start | bytes 1425416 | tf_op jit(solution)/shard_map/ppermute | solution.py:24
  98.2 0.6 pad_add_fusion.place_ref
  98.8 1.5 %collective-permute-done.6.refs_3_ = bf16[928,256]{1,0:T(8,128)(2,1)} collective-permute-done((bf16[928,256]{1,0:T(8,128)(2,1)}, bf16[928,256]{1,0:T(8,128)(2,1)}, u32[]{:S(2)}, u32[]{:S(2)}) %collective-permute-start.6) | collective-permute-done | bytes 475168 | tf_op jit(solution)/shard_map/ppermute | solution.py:24
  100.4 0.0 collective-permute-done.10.refs_5_
  100.4 0.0 collective-permute-done.4.refs_1_
  100.4 2.6 %all-gather.2.cloned.1.call-done = bf16[8192,256]{1,0:T(8,128)(2,1)} async-done(((bf16[1024,256]{1,0:T(8,128)(2,1)}), bf16[8192,256]{1,0:T(8,128)(2,1)}) %all-gather.2.cloned.1.call-update) | async-done | bytes 4194320 | tf_op jit(solution)/shard_map/all_gather | solution.py:147
  102.9 0.0 copy-done
  102.9 0.0 copy-done.1
  102.9 7.8 %shard_map.37 = bf16[924,512]{1,0:T(8,128)(2,1)} custom-call(s32[3]{0:T(128)} %pad_add_fusion.place_ref, s32[16]{0:T(128)} %counts_ref.1, bf16[4,928,256]{2,1,0:T(8,128)(2,1)} %copy-done, bf16[4,928,256]{2,1,0:T(8,128)(2,1)} %collective-permute-done.4.refs_1_, bf16[928,256]{1,0:T(8,128)(2,1)} %collective-permute-done.5.refs_2_, ...), custom_call_target="tpu_custom_call" | custom-call | flops 3892314112 | bytes 13631488 | tf_op jit(solution)/shard_map/pallas_call | solution.py:118
Async XLA Ops:
  6.5 96.4 %all-gather.2.cloned.1.call-start = ((), (), s32[]{:S(2)}) async-start(), calls=%async_computation | async-start | bytes 4718592 | tf_op jit(solution)/shard_map/all_gather | solution.py:147
  6.5 9.9 %collective-permute-start = (bf16[256,256]{1,0:T(8,128)(2,1)}, bf16[256,256]{1,0:T(8,128)(2,1)S(1)}, u32[]{:S(2)}, u32[]{:S(2)}) collective-permute-start(bf16[256,256]{1,0:T(8,128)(2,1)} %param.4), channel_id=1, source_target_pairs={{0,0},{1,8},{2,16},{3,24},{4,4},{5,12},{6,20},{7,28},{8,1},{9,9},{... | collective-permute-start | bytes 393224 | tf_op jit(solution)/shard_map/ppermute | solution.py:24
  31.1 25.6 %collective-permute-start.5 = (bf16[928,256]{1,0:T(8,128)(2,1)S(1)}, bf16[928,256]{1,0:T(8,128)(2,1)}, u32[]{:S(2)}, u32[]{:S(2)}) collective-permute-start(bf16[928,256]{1,0:T(8,128)(2,1)S(1)} %pad.4), channel_id=1, source_target_pairs={{0,2},{1,3},{2,0},{3,1},{4,6},{5,7},{6,4},{7,5},{8,10},{9,11},{10,... | collective-permute-start | bytes 1425416 | tf_op jit(solution)/shard_map/ppermute | solution.py:24
  39.7 33.6 %collective-permute-start.3 = (bf16[928,256]{1,0:T(8,128)(2,1)S(1)}, bf16[928,256]{1,0:T(8,128)(2,1)S(1)}, u32[]{:S(2)}, u32[]{:S(2)}) collective-permute-start(bf16[928,256]{1,0:T(8,128)(2,1)S(1)} %pad.4), channel_id=1, source_target_pairs={{0,256},{1,257},{2,258},{3,259},{4,260},{5,261},{6,262},{7,263},{8... | collective-permute-start | bytes 1425416 | tf_op jit(solution)/shard_map/ppermute | solution.py:24
  51.4 24.4 %collective-permute-start.2 = (bf16[928,256]{1,0:T(8,128)(2,1)S(1)}, bf16[928,256]{1,0:T(8,128)(2,1)S(1)}, u32[]{:S(2)}, u32[]{:S(2)}) collective-permute-start(bf16[928,256]{1,0:T(8,128)(2,1)S(1)} %pad.4), channel_id=1, source_target_pairs={{0,384},{1,385},{2,386},{3,387},{4,388},{5,389},{6,390},{7,391},{8... | collective-permute-start | bytes 1425416 | tf_op jit(solution)/shard_map/ppermute | solution.py:24
  53.4 22.4 %collective-permute-start.1 = (bf16[928,256]{1,0:T(8,128)(2,1)S(1)}, bf16[928,256]{1,0:T(8,128)(2,1)S(1)}, u32[]{:S(2)}, u32[]{:S(2)}) collective-permute-start(bf16[928,256]{1,0:T(8,128)(2,1)S(1)} %pad.4), channel_id=1, source_target_pairs={{0,128},{1,129},{2,130},{3,131},{4,132},{5,133},{6,134},{7,135},{8... | collective-permute-start | bytes 1425416 | tf_op jit(solution)/shard_map/ppermute | solution.py:24
  56.7 25.7 %collective-permute-start.9 = (bf16[928,256]{1,0:T(8,128)(2,1)}, bf16[928,256]{1,0:T(8,128)(2,1)S(1)}, u32[]{:S(2)}, u32[]{:S(2)}) collective-permute-start(bf16[928,256]{1,0:T(8,128)(2,1)} %collective-permute-done.5.refs_2_), channel_id=1, source_target_pairs={{0,256},{1,257},{2,258},{3,259},{4,260},{5,261},{6,262},{7,263},{8... | collective-permute-start | bytes 1425416 | tf_op jit(solution)/shard_map/ppermute | solution.py:24
  64.6 28.2 %collective-permute-start.8 = (bf16[928,256]{1,0:T(8,128)(2,1)}, bf16[928,256]{1,0:T(8,128)(2,1)S(1)}, u32[]{:S(2)}, u32[]{:S(2)}) collective-permute-start(bf16[928,256]{1,0:T(8,128)(2,1)} %collective-permute-done.5.refs_2_), channel_id=1, source_target_pairs={{0,384},{1,385},{2,386},{3,387},{4,388},{5,389},{6,390},{7,391},{8... | collective-permute-start | bytes 1425416 | tf_op jit(solution)/shard_map/ppermute | solution.py:24
  73.3 20.1 %collective-permute-start.7 = (bf16[928,256]{1,0:T(8,128)(2,1)}, bf16[928,256]{1,0:T(8,128)(2,1)S(1)}, u32[]{:S(2)}, u32[]{:S(2)}) collective-permute-start(bf16[928,256]{1,0:T(8,128)(2,1)} %collective-permute-done.5.refs_2_), channel_id=1, source_target_pairs={{0,128},{1,129},{2,130},{3,131},{4,132},{5,133},{6,134},{7,135},{8... | collective-permute-start | bytes 1425416 | tf_op jit(solution)/shard_map/ppermute | solution.py:24
  76.1 26.8 %copy-start = (bf16[4,928,256]{2,1,0:T(8,128)(2,1)}, bf16[4,928,256]{2,1,0:T(8,128)(2,1)S(1)}, u32[]{:S(2)}) copy-start(bf16[4,928,256]{2,1,0:T(8,128)(2,1)S(1)} %pad_maximum_fusion.refs_0_) | copy-start | bytes 5701636
  76.1 24.3 %collective-permute-start.4 = (bf16[4,928,256]{2,1,0:T(8,128)(2,1)S(1)}, bf16[4,928,256]{2,1,0:T(8,128)(2,1)}, u32[]{:S(2)}, u32[]{:S(2)}) collective-permute-start(bf16[4,928,256]{2,1,0:T(8,128)(2,1)S(1)} %pad_maximum_fusion.refs_0_), channel_id=1, source_target_pairs={{0,1},{1,0},{2,3},{3,2},{4,5},{5,4},{6,7},{7,6},{8,9},{9,8},{10,11... | collective-permute-start | bytes 5701640 | tf_op jit(solution)/shard_map/ppermute | solution.py:24
  93.6 9.3 %copy-start.1 = (bf16[3,928,256]{2,1,0:T(8,128)(2,1)}, bf16[3,928,256]{2,1,0:T(8,128)(2,1)S(1)}, u32[]{:S(2)}) copy-start(bf16[3,928,256]{2,1,0:T(8,128)(2,1)S(1)} %pad_maximum_fusion.1.refs_4_) | copy-start | bytes 4276228
  93.6 6.7 %collective-permute-start.10 = (bf16[3,928,256]{2,1,0:T(8,128)(2,1)S(1)}, bf16[3,928,256]{2,1,0:T(8,128)(2,1)}, u32[]{:S(2)}, u32[]{:S(2)}) collective-permute-start(bf16[3,928,256]{2,1,0:T(8,128)(2,1)S(1)} %pad_maximum_fusion.1.refs_4_), channel_id=1, source_target_pairs={{0,1},{1,0},{2,3},{3,2},{4,5},{5,4},{6,7},{7,6},{8,9},{9,8},{10,11... | collective-permute-start | bytes 4276232 | tf_op jit(solution)/shard_map/ppermute | solution.py:24
  96.3 4.1 %collective-permute-start.6 = (bf16[928,256]{1,0:T(8,128)(2,1)}, bf16[928,256]{1,0:T(8,128)(2,1)}, u32[]{:S(2)}, u32[]{:S(2)}) collective-permute-start(bf16[928,256]{1,0:T(8,128)(2,1)} %collective-permute-done.5.refs_2_), channel_id=1, source_target_pairs={{0,1},{1,0},{2,3},{3,2},{4,5},{5,4},{6,7},{7,6},{8,9},{9,8},{10,11... | collective-permute-start | bytes 1425416 | tf_op jit(solution)/shard_map/ppermute | solution.py:24
Sparse Core Ops, SparseCore 0:
  31.3 71.6 all-gather.1

commit v6 on v5

--- a/solution.py
+++ b/solution.py
@@ -10,7 +10,7 @@
 ROWBLK = 128
 MROWS = 256
 VMEM = 60 << 20
-AHEAD = 3
+AHEAD = 4
 NX, NZ, NYL, NYH, NC = 4, 8, 4, 2, 2
 ALL = ("x", "z", "yl", "yh", "c")
 PLACES = list(itertools.product(range(NX), range(NZ), range(NYL), range(NYH), range(NC)))

time: 118 us -> 118 us (level)
  no operation moved by 1% of the time
where the time goes in v6:
time: 118 us; the launch traced here: 117 us
  starting transfers between devices  59.4 us (50%)
  waiting for transfers between devices  20 us (17%)
  blocking collectives  14.7 us (12%)
  between operations  13.6 us (12%)
  Pallas kernels  7.61 us (6%)
    ppermute x11, starting transfers between devices, permute(): lax.ppermute(value, ALL, [(linear(*p), linear(*target(*p))) for p in PLAC...  59.4 us
    ppermute x11, waiting for transfers between devices, permute(): lax.ppermute(value, ALL, [(linear(*p), linear(*target(*p))) for p in PLAC...  17.5 us
    all_gather x1, blocking collectives, shards(): piece = lax.all_gather(near, 'yl', axis=0, tiled=True)  14.7 us
    pallas_call x1, Pallas kernels, product(): pl.pallas_call(kernel, out_shape=jax.ShapeDtypeStruct((width, cols), jnp....  7.61 us
    all_gather x1, waiting for transfers between devices, shards(): lax.all_gather(piece, 'z', axis=0, tiled=True)  2.56 us
  transfers between devices with their start and end apart: 12, of which 6 were waited for; matrix products, arithmetic and copies ran while one was open for 2% of the time, Pallas kernels for 0%

profile of v6, /device:TPU:1, one launch (start us, length us, event | category | flops | bytes accessed | tf_op | source)
XLA Modules:
  0.0 117.4 jit_solution(511432155943436484)
XLA Ops:
  6.5 0.0 all-gather.2.cloned.1.call-start
  6.5 5.6 %collective-permute-start = (bf16[256,256]{1,0:T(8,128)(2,1)}, bf16[256,256]{1,0:T(8,128)(2,1)S(1)}, u32[]{:S(2)}, u32[]{:S(2)}) collective-permute-start(bf16[256,256]{1,0:T(8,128)(2,1)} %param.4), channel_id=1, source_target_pairs={{0,0},{1,8},{2,16},{3,24},{4,4},{5,12},{6,20},{7,28},{8,1},{9,9},{... | collective-permute-start | bytes 393224 | tf_op jit(solution)/shard_map/ppermute | solution.py:24
  12.1 1.1 pad.4
  13.2 3.2 %collective-permute-done = bf16[256,256]{1,0:T(8,128)(2,1)S(1)} collective-permute-done((bf16[256,256]{1,0:T(8,128)(2,1)}, bf16[256,256]{1,0:T(8,128)(2,1)S(1)}, u32[]{:S(2)}, u32[]{:S(2)}) %collective-permute-start) | collective-permute-done | bytes 131104 | tf_op jit(solution)/shard_map/ppermute | solution.py:24
  16.4 14.7 %all_gather.6 = bf16[1024,256]{1,0:T(8,128)(2,1)} all-gather(bf16[256,256]{1,0:T(8,128)(2,1)S(1)} %collective-permute-done), channel_id=1, replica_groups=mesh['x'=4,'z'=8,'yl'=4,'yh'=2,'c'=2] {'yl'}, dimensions={0}, use_global_device_ids=true | all-gather | bytes 655360 | tf_op jit(solution)/shard_map/all_gather | solution.py:146
  31.1 0.0 all-gather.2.cloned.1.call-update
  31.1 8.6 %collective-permute-start.5 = (bf16[928,256]{1,0:T(8,128)(2,1)S(1)}, bf16[928,256]{1,0:T(8,128)(2,1)}, u32[]{:S(2)}, u32[]{:S(2)}) collective-permute-start(bf16[928,256]{1,0:T(8,128)(2,1)S(1)} %pad.4), channel_id=1, source_target_pairs={{0,2},{1,3},{2,0},{3,1},{4,6},{5,7},{6,4},{7,5},{8,10},{9,11},{10,... | collective-permute-start | bytes 1425416 | tf_op jit(solution)/shard_map/ppermute | solution.py:24
  39.7 11.7 %collective-permute-start.3 = (bf16[928,256]{1,0:T(8,128)(2,1)S(1)}, bf16[928,256]{1,0:T(8,128)(2,1)S(1)}, u32[]{:S(2)}, u32[]{:S(2)}) collective-permute-start(bf16[928,256]{1,0:T(8,128)(2,1)S(1)} %pad.4), channel_id=1, source_target_pairs={{0,256},{1,257},{2,258},{3,259},{4,260},{5,261},{6,262},{7,263},{8... | collective-permute-start | bytes 1425416 | tf_op jit(solution)/shard_map/ppermute | solution.py:24
  51.4 1.9 %collective-permute-start.2 = (bf16[928,256]{1,0:T(8,128)(2,1)S(1)}, bf16[928,256]{1,0:T(8,128)(2,1)S(1)}, u32[]{:S(2)}, u32[]{:S(2)}) collective-permute-start(bf16[928,256]{1,0:T(8,128)(2,1)S(1)} %pad.4), channel_id=1, source_target_pairs={{0,384},{1,385},{2,386},{3,387},{4,388},{5,389},{6,390},{7,391},{8... | collective-permute-start | bytes 1425416 | tf_op jit(solution)/shard_map/ppermute | solution.py:24
  53.4 3.4 %collective-permute-start.1 = (bf16[928,256]{1,0:T(8,128)(2,1)S(1)}, bf16[928,256]{1,0:T(8,128)(2,1)S(1)}, u32[]{:S(2)}, u32[]{:S(2)}) collective-permute-start(bf16[928,256]{1,0:T(8,128)(2,1)S(1)} %pad.4), channel_id=1, source_target_pairs={{0,128},{1,129},{2,130},{3,131},{4,132},{5,133},{6,134},{7,135},{8... | collective-permute-start | bytes 1425416 | tf_op jit(solution)/shard_map/ppermute | solution.py:24
  56.7 0.0 collective-permute-done.5.refs_2_
  56.7 7.8 %collective-permute-start.9 = (bf16[928,256]{1,0:T(8,128)(2,1)}, bf16[928,256]{1,0:T(8,128)(2,1)S(1)}, u32[]{:S(2)}, u32[]{:S(2)}) collective-permute-start(bf16[928,256]{1,0:T(8,128)(2,1)} %collective-permute-done.5.refs_2_), channel_id=1, source_target_pairs={{0,256},{1,257},{2,258},{3,259},{4,260},{5,261},{6,262},{7,263},{8... | collective-permute-start | bytes 1425416 | tf_op jit(solution)/shard_map/ppermute | solution.py:24
  64.6 8.7 %collective-permute-start.8 = (bf16[928,256]{1,0:T(8,128)(2,1)}, bf16[928,256]{1,0:T(8,128)(2,1)S(1)}, u32[]{:S(2)}, u32[]{:S(2)}) collective-permute-start(bf16[928,256]{1,0:T(8,128)(2,1)} %collective-permute-done.5.refs_2_), channel_id=1, source_target_pairs={{0,384},{1,385},{2,386},{3,387},{4,388},{5,389},{6,390},{7,391},{8... | collective-permute-start | bytes 1425416 | tf_op jit(solution)/shard_map/ppermute | solution.py:24
  73.3 0.0 collective-permute-done.3
  73.3 2.5 %collective-permute-start.7 = (bf16[928,256]{1,0:T(8,128)(2,1)}, bf16[928,256]{1,0:T(8,128)(2,1)S(1)}, u32[]{:S(2)}, u32[]{:S(2)}) collective-permute-start(bf16[928,256]{1,0:T(8,128)(2,1)} %collective-permute-done.5.refs_2_), channel_id=1, source_target_pairs={{0,128},{1,129},{2,130},{3,131},{4,132},{5,133},{6,134},{7,135},{8... | collective-permute-start | bytes 1425416 | tf_op jit(solution)/shard_map/ppermute | solution.py:24
  75.8 0.0 collective-permute-done.2
  75.8 0.0 collective-permute-done.1
  75.8 0.2 pad_maximum_fusion.refs_0_
  76.1 0.0 copy-start
  76.1 4.6 %collective-permute-start.4 = (bf16[4,928,256]{2,1,0:T(8,128)(2,1)S(1)}, bf16[4,928,256]{2,1,0:T(8,128)(2,1)}, u32[]{:S(2)}, u32[]{:S(2)}) collective-permute-start(bf16[4,928,256]{2,1,0:T(8,128)(2,1)S(1)} %pad_maximum_fusion.refs_0_), channel_id=1, source_target_pairs={{0,1},{1,0},{2,3},{3,2},{4,5},{5,4},{6,7},{7,6},{8,9},{9,8},{10,11... | collective-permute-start | bytes 5701640 | tf_op jit(solution)/shard_map/ppermute | solution.py:24
  80.7 1.8 %collective-permute-done.9 = bf16[928,256]{1,0:T(8,128)(2,1)S(1)} collective-permute-done((bf16[928,256]{1,0:T(8,128)(2,1)}, bf16[928,256]{1,0:T(8,128)(2,1)S(1)}, u32[]{:S(2)}, u32[]{:S(2)}) %collective-permute-start.9) | collective-permute-done | bytes 475168 | tf_op jit(solution)/shard_map/ppermute | solution.py:24
  82.5 10.3 %collective-permute-done.8 = bf16[928,256]{1,0:T(8,128)(2,1)S(1)} collective-permute-done((bf16[928,256]{1,0:T(8,128)(2,1)}, bf16[928,256]{1,0:T(8,128)(2,1)S(1)}, u32[]{:S(2)}, u32[]{:S(2)}) %collective-permute-start.8) | collective-permute-done | bytes 475168 | tf_op jit(solution)/shard_map/ppermute | solution.py:24
  92.7 0.7 collective-permute-done.7
  93.5 0.2 pad_maximum_fusion.1.refs_4_
  93.6 0.0 copy-start.1
  93.6 2.6 %collective-permute-start.10 = (bf16[3,928,256]{2,1,0:T(8,128)(2,1)S(1)}, bf16[3,928,256]{2,1,0:T(8,128)(2,1)}, u32[]{:S(2)}, u32[]{:S(2)}) collective-permute-start(bf16[3,928,256]{2,1,0:T(8,128)(2,1)S(1)} %pad_maximum_fusion.1.refs_4_), channel_id=1, source_target_pairs={{0,1},{1,0},{2,3},{3,2},{4,5},{5,4},{6,7},{7,6},{8,9},{9,8},{10,11... | collective-permute-start | bytes 4276232 | tf_op jit(solution)/shard_map/ppermute | solution.py:24
  96.3 1.9 %collective-permute-start.6 = (bf16[928,256]{1,0:T(8,128)(2,1)}, bf16[928,256]{1,0:T(8,128)(2,1)}, u32[]{:S(2)}, u32[]{:S(2)}) collective-permute-start(bf16[928,256]{1,0:T(8,128)(2,1)} %collective-permute-done.5.refs_2_), channel_id=1, source_target_pairs={{0,1},{1,0},{2,3},{3,2},{4,5},{5,4},{6,7},{7,6},{8,9},{9,8},{10,11... | collective-permute-start | bytes 1425416 | tf_op jit(solution)/shard_map/ppermute | solution.py:24
  98.2 0.6 pad_add_fusion.place_ref
  98.8 1.5 %collective-permute-done.6.refs_3_ = bf16[928,256]{1,0:T(8,128)(2,1)} collective-permute-done((bf16[928,256]{1,0:T(8,128)(2,1)}, bf16[928,256]{1,0:T(8,128)(2,1)}, u32[]{:S(2)}, u32[]{:S(2)}) %collective-permute-start.6) | collective-permute-done | bytes 475168 | tf_op jit(solution)/shard_map/ppermute | solution.py:24
  100.4 0.0 collective-permute-done.10.refs_5_
  100.4 0.0 collective-permute-done.4.refs_1_
  100.4 2.6 %all-gather.2.cloned.1.call-done = bf16[8192,256]{1,0:T(8,128)(2,1)} async-done(((bf16[1024,256]{1,0:T(8,128)(2,1)}), bf16[8192,256]{1,0:T(8,128)(2,1)}) %all-gather.2.cloned.1.call-update) | async-done | bytes 4194320 | tf_op jit(solution)/shard_map/all_gather | solution.py:147
  102.9 0.0 copy-done
  102.9 0.0 copy-done.1
  102.9 7.6 %shard_map.37 = bf16[924,512]{1,0:T(8,128)(2,1)} custom-call(s32[3]{0:T(128)} %pad_add_fusion.place_ref, s32[16]{0:T(128)} %counts_ref.1, bf16[4,928,256]{2,1,0:T(8,128)(2,1)} %copy-done, bf16[4,928,256]{2,1,0:T(8,128)(2,1)} %collective-permute-done.4.refs_1_, bf16[928,256]{1,0:T(8,128)(2,1)} %collective-permute-done.5.refs_2_, ...), custom_call_target="tpu_custom_call" | custom-call | flops 3892314112 | bytes 13631488 | tf_op jit(solution)/shard_map/pallas_call | solution.py:118
Async XLA Ops:
  6.5 96.4 %all-gather.2.cloned.1.call-start = ((), (), s32[]{:S(2)}) async-start(), calls=%async_computation | async-start | bytes 4718592 | tf_op jit(solution)/shard_map/all_gather | solution.py:147
  6.5 9.9 %collective-permute-start = (bf16[256,256]{1,0:T(8,128)(2,1)}, bf16[256,256]{1,0:T(8,128)(2,1)S(1)}, u32[]{:S(2)}, u32[]{:S(2)}) collective-permute-start(bf16[256,256]{1,0:T(8,128)(2,1)} %param.4), channel_id=1, source_target_pairs={{0,0},{1,8},{2,16},{3,24},{4,4},{5,12},{6,20},{7,28},{8,1},{9,9},{... | collective-permute-start | bytes 393224 | tf_op jit(solution)/shard_map/ppermute | solution.py:24
  31.1 25.6 %collective-permute-start.5 = (bf16[928,256]{1,0:T(8,128)(2,1)S(1)}, bf16[928,256]{1,0:T(8,128)(2,1)}, u32[]{:S(2)}, u32[]{:S(2)}) collective-permute-start(bf16[928,256]{1,0:T(8,128)(2,1)S(1)} %pad.4), channel_id=1, source_target_pairs={{0,2},{1,3},{2,0},{3,1},{4,6},{5,7},{6,4},{7,5},{8,10},{9,11},{10,... | collective-permute-start | bytes 1425416 | tf_op jit(solution)/shard_map/ppermute | solution.py:24
  39.7 33.6 %collective-permute-start.3 = (bf16[928,256]{1,0:T(8,128)(2,1)S(1)}, bf16[928,256]{1,0:T(8,128)(2,1)S(1)}, u32[]{:S(2)}, u32[]{:S(2)}) collective-permute-start(bf16[928,256]{1,0:T(8,128)(2,1)S(1)} %pad.4), channel_id=1, source_target_pairs={{0,256},{1,257},{2,258},{3,259},{4,260},{5,261},{6,262},{7,263},{8... | collective-permute-start | bytes 1425416 | tf_op jit(solution)/shard_map/ppermute | solution.py:24
  51.4 24.4 %collective-permute-start.2 = (bf16[928,256]{1,0:T(8,128)(2,1)S(1)}, bf16[928,256]{1,0:T(8,128)(2,1)S(1)}, u32[]{:S(2)}, u32[]{:S(2)}) collective-permute-start(bf16[928,256]{1,0:T(8,128)(2,1)S(1)} %pad.4), channel_id=1, source_target_pairs={{0,384},{1,385},{2,386},{3,387},{4,388},{5,389},{6,390},{7,391},{8... | collective-permute-start | bytes 1425416 | tf_op jit(solution)/shard_map/ppermute | solution.py:24
  53.4 22.4 %collective-permute-start.1 = (bf16[928,256]{1,0:T(8,128)(2,1)S(1)}, bf16[928,256]{1,0:T(8,128)(2,1)S(1)}, u32[]{:S(2)}, u32[]{:S(2)}) collective-permute-start(bf16[928,256]{1,0:T(8,128)(2,1)S(1)} %pad.4), channel_id=1, source_target_pairs={{0,128},{1,129},{2,130},{3,131},{4,132},{5,133},{6,134},{7,135},{8... | collective-permute-start | bytes 1425416 | tf_op jit(solution)/shard_map/ppermute | solution.py:24
  56.7 25.7 %collective-permute-start.9 = (bf16[928,256]{1,0:T(8,128)(2,1)}, bf16[928,256]{1,0:T(8,128)(2,1)S(1)}, u32[]{:S(2)}, u32[]{:S(2)}) collective-permute-start(bf16[928,256]{1,0:T(8,128)(2,1)} %collective-permute-done.5.refs_2_), channel_id=1, source_target_pairs={{0,256},{1,257},{2,258},{3,259},{4,260},{5,261},{6,262},{7,263},{8... | collective-permute-start | bytes 1425416 | tf_op jit(solution)/shard_map/ppermute | solution.py:24
  64.6 28.2 %collective-permute-start.8 = (bf16[928,256]{1,0:T(8,128)(2,1)}, bf16[928,256]{1,0:T(8,128)(2,1)S(1)}, u32[]{:S(2)}, u32[]{:S(2)}) collective-permute-start(bf16[928,256]{1,0:T(8,128)(2,1)} %collective-permute-done.5.refs_2_), channel_id=1, source_target_pairs={{0,384},{1,385},{2,386},{3,387},{4,388},{5,389},{6,390},{7,391},{8... | collective-permute-start | bytes 1425416 | tf_op jit(solution)/shard_map/ppermute | solution.py:24
  73.3 20.1 %collective-permute-start.7 = (bf16[928,256]{1,0:T(8,128)(2,1)}, bf16[928,256]{1,0:T(8,128)(2,1)S(1)}, u32[]{:S(2)}, u32[]{:S(2)}) collective-permute-start(bf16[928,256]{1,0:T(8,128)(2,1)} %collective-permute-done.5.refs_2_), channel_id=1, source_target_pairs={{0,128},{1,129},{2,130},{3,131},{4,132},{5,133},{6,134},{7,135},{8... | collective-permute-start | bytes 1425416 | tf_op jit(solution)/shard_map/ppermute | solution.py:24
  76.1 26.8 %copy-start = (bf16[4,928,256]{2,1,0:T(8,128)(2,1)}, bf16[4,928,256]{2,1,0:T(8,128)(2,1)S(1)}, u32[]{:S(2)}) copy-start(bf16[4,928,256]{2,1,0:T(8,128)(2,1)S(1)} %pad_maximum_fusion.refs_0_) | copy-start | bytes 5701636
  76.1 24.3 %collective-permute-start.4 = (bf16[4,928,256]{2,1,0:T(8,128)(2,1)S(1)}, bf16[4,928,256]{2,1,0:T(8,128)(2,1)}, u32[]{:S(2)}, u32[]{:S(2)}) collective-permute-start(bf16[4,928,256]{2,1,0:T(8,128)(2,1)S(1)} %pad_maximum_fusion.refs_0_), channel_id=1, source_target_pairs={{0,1},{1,0},{2,3},{3,2},{4,5},{5,4},{6,7},{7,6},{8,9},{9,8},{10,11... | collective-permute-start | bytes 5701640 | tf_op jit(solution)/shard_map/ppermute | solution.py:24
  93.6 9.3 %copy-start.1 = (bf16[3,928,256]{2,1,0:T(8,128)(2,1)}, bf16[3,928,256]{2,1,0:T(8,128)(2,1)S(1)}, u32[]{:S(2)}) copy-start(bf16[3,928,256]{2,1,0:T(8,128)(2,1)S(1)} %pad_maximum_fusion.1.refs_4_) | copy-start | bytes 4276228
  93.6 6.7 %collective-permute-start.10 = (bf16[3,928,256]{2,1,0:T(8,128)(2,1)S(1)}, bf16[3,928,256]{2,1,0:T(8,128)(2,1)}, u32[]{:S(2)}, u32[]{:S(2)}) collective-permute-start(bf16[3,928,256]{2,1,0:T(8,128)(2,1)S(1)} %pad_maximum_fusion.1.refs_4_), channel_id=1, source_target_pairs={{0,1},{1,0},{2,3},{3,2},{4,5},{5,4},{6,7},{7,6},{8,9},{9,8},{10,11... | collective-permute-start | bytes 4276232 | tf_op jit(solution)/shard_map/ppermute | solution.py:24
  96.3 4.1 %collective-permute-start.6 = (bf16[928,256]{1,0:T(8,128)(2,1)}, bf16[928,256]{1,0:T(8,128)(2,1)}, u32[]{:S(2)}, u32[]{:S(2)}) collective-permute-start(bf16[928,256]{1,0:T(8,128)(2,1)} %collective-permute-done.5.refs_2_), channel_id=1, source_target_pairs={{0,1},{1,0},{2,3},{3,2},{4,5},{5,4},{6,7},{7,6},{8,9},{9,8},{10,11... | collective-permute-start | bytes 1425416 | tf_op jit(solution)/shard_map/ppermute | solution.py:24
Sparse Core Ops, SparseCore 0:
  31.3 71.6 all-gather.1
